TPU v7x, 32 devices: a whole 2x2x4 slice. The times are simulated.
32 devices in a mesh: expert: 8 (over y, x, core), hidden: 4 (over z).
Axes of the slice: x: 2, y: 2, z: 4, core: 2. Of those that a mesh axis runs over, the one named last changes fastest.
Arguments:
- tokens: bfloat16 [16384, 768], P(('expert', 'hidden')), may hold values from -6 to 6
- cotangent: bfloat16 [16384, 768], P(('expert', 'hidden')), may hold values from -6 to 6
- segments: int32 [32, 512], P(('expert', 'hidden')), may hold values from 0 to 7, never falling along the last dimension, each value on 1 to 256 neighbouring positions
- routes: int32 [16384], P(('expert', 'hidden')), may hold values from 0 to 15
- slot_ids: int32 [16384], P(('expert', 'hidden')), may hold values from 0 to 39, as said below
- kept_flags: int32 [16384], P(('expert', 'hidden')), may hold values from 0 to 1, as said below
- gain_one: float32 [768], replicated, may hold values from 0.1 to 1.9
- w_qkv: bfloat16 [768, 2304], replicated, may hold values from -0.21875 to 0.21875
- w_out: bfloat16 [768, 768], replicated, may hold values from -0.875 to 0.875
- bias_table: float32 [32, 12], replicated, may hold values from -4 to 4
- gain_two: float32 [768], replicated, may hold values from 0.1 to 1.9
- w_router: float32 [768, 16], replicated, may hold values from -0.109375 to 0.109375
- w_in: bfloat16 [16, 768, 3072], P('expert', None, 'hidden'), may hold values from -0.21875 to 0.21875
- w_back: bfloat16 [16, 3072, 768], P('expert', 'hidden'), may hold values from -3 to 3
Outputs:
- output: bfloat16 [16384, 768], P(('expert', 'hidden'))
- grad_tokens: float32 [16384, 768], P(('expert', 'hidden'))
- grad_gain_one: float32 [768], replicated
- grad_w_qkv: float32 [768, 2304], replicated
- grad_w_out: float32 [768, 768], replicated
- grad_bias: float32 [32, 12], replicated
- grad_gain_two: float32 [768], replicated
- grad_router: float32 [768, 16], replicated
- grad_w_in: float32 [16, 768, 3072], P('expert', None, 'hidden')
- grad_w_back: float32 [16, 3072, 768], P('expert', 'hidden')
Inputs may be any that keep to these rules, and one draw needn't show every extreme that they name: `slot_ids`: among the tokens of one device (aligned blocks of 512) that name one expert, the kept ones hold slots 0, 1, 2, ... in token order and at most 40 are kept; later ones are dropped and hold slot 39. In every draw some expert gets more than 40 tokens from every device. `kept_flags`: 1 exactly where the token's place among its device's tokens for its expert is below 40. `segments`: ids are per packed row and never fall along it.
All inputs are finite; a program needn't handle non-finite values.
Results may differ from a plain program's by a relative error of at most 0.014.
Values may be sent and summed in bfloat16 or wider, within the bound.
No kernel may reach another device: no remote copies, remote signals or barrier semaphores. Data moves between devices by JAX's collectives and lax.ppermute only.
A program may use at most 320 MiB of HBM per device.

v0:
```python
import functools

import jax
import jax.numpy as jnp
from jax import lax
from jax.experimental import pallas as pl
from jax.experimental.pallas import tpu as pltpu
from jax.sharding import PartitionSpec as P

eps = 1e-06
bucket_edges = (12, 16, 23, 32, 46, 64, 91)
highest = lax.Precision.HIGHEST
f32 = jnp.float32
bf16 = jnp.bfloat16
i32 = jnp.int32
BLOCK = 128
VMEM_BYTES = 56 << 20
NN = (((1,), (0,)), ((), ()))
NT = (((1,), (1,)), ((), ()))
TN = (((0,), (0,)), ((), ()))


def mm(left, right, dims=NN):
    return lax.dot_general(left, right, dims, preferred_element_type=f32)


def mm_exact(left, right, dims=NN):
    return lax.dot_general(left, right, dims, precision=highest, preferred_element_type=f32)


def split(values):
    high = values.astype(bf16)
    return high, (values - high.astype(f32)).astype(bf16)


def params(semantics=None):
    if semantics is None:
        return pltpu.CompilerParams(vmem_limit_bytes=VMEM_BYTES)
    return pltpu.CompilerParams(vmem_limit_bytes=VMEM_BYTES, dimension_semantics=semantics)


def cost(flops, moved):
    return pl.CostEstimate(
        flops=int(flops) // 100, bytes_accessed=int(moved) // 100, transcendentals=0
    )


def bucket_of(offset):
    distance = jnp.abs(offset)
    coarse = jnp.full_like(distance, 8)
    for edge_value in bucket_edges:
        coarse = coarse + (distance >= edge_value).astype(i32)
    return jnp.where(distance < 8, distance, coarse) + 16 * (offset > 0).astype(i32)


def one_hot(mask):
    return mask.astype(f32).astype(bf16)


def lane_numbers(rows, width):
    return lax.broadcasted_iota(i32, (rows, width), 1)


def place_kernel(routes_ref, slot_ref, kept_ref, seg_ref, bias_ref, row_ref, col_ref, diag_ref, *, capacity, local_experts):
    tokens = seg_ref.shape[1]
    routes = routes_ref[...]
    seat = (routes // local_experts) * capacity + slot_ref[...]
    kept = kept_ref[...] == 1
    line = lax.broadcasted_iota(i32, (BLOCK, tokens), 0)
    stacked = jnp.where(line == local_experts, routes, 0)
    stacked = jnp.where(line == local_experts + 1, seg_ref[...], stacked)
    for le in range(local_experts):
        key = jnp.where(kept & (routes % local_experts == le), seat, -1)
        stacked = jnp.where(line == le, key, stacked)
    row_ref[...] = stacked[: row_ref.shape[0]]
    col_ref[...] = stacked.T
    buckets = bias_ref.shape[0]
    offset = lane_numbers(buckets, 4 * BLOCK) - 2 * BLOCK
    pick = bucket_of(offset) == lax.broadcasted_iota(i32, (buckets, 4 * BLOCK), 0)
    diag_ref[...] = mm_exact(bias_ref[...], pick.astype(f32), TN)


def slots_kernel(place_ref, *refs, parts, le):
    key_refs = refs[:parts]
    rows_ref, out_ref = refs[parts:]
    direct = len(out_ref.shape) == 4
    slots = out_ref.shape[0] * out_ref.shape[2] if direct else out_ref.shape[1]
    tokens = rows_ref.shape[1]
    for j in range(parts):
        whole = (place_ref[0] + j) % parts
        key = key_refs[j][le : le + 1, :]
        table = lax.broadcasted_iota(i32, (slots, tokens), 0) == key
        rows = mm(one_hot(table), rows_ref[whole])
        if direct:
            by_group(rows, out_ref, whole)
        else:
            out_ref[whole] = rows.astype(bf16)


def by_group(rows, out_ref, place):
    capacity = out_ref.shape[2]
    for group in range(out_ref.shape[0]):
        piece = rows[group * capacity : (group + 1) * capacity]
        out_ref[group, place] = piece.astype(bf16)


def qkv_kernel(tok_ref, gain_ref, w_ref, qkv_ref, turned_ref, low_ref):
    @pl.when(pl.program_id(0) == 0)
    def _():
        values = tok_ref[...].astype(f32)
        inverse = lax.rsqrt(jnp.mean(values * values, axis=-1, keepdims=True) + eps)
        normed = values * inverse * gain_ref[...]
        low_ref[...] = normed.astype(bf16)
        turned_ref[...] = normed.T.astype(bf16)

    qkv_ref[...] = mm(low_ref[...], w_ref[...]).astype(bf16)


def attend_kernel(q_ref, k_ref, v_ref, row_ids_ref, cols_ref, diag_ref, att_ref, probs_ref, *, seg_line, head_start):
    length = k_ref.shape[0]
    blocks = length // BLOCK
    lane = lane_numbers(1, BLOCK)
    half = BLOCK // 2
    scale = half**-0.5
    keys = k_ref[...]
    vals = v_ref[...]
    row_ids = row_ids_ref[seg_line : seg_line + 1, :]
    bias_tiles = []
    for s in range(2):
        diag = diag_ref[pl.ds(head_start + 2 * pl.program_id(0) + s, 1), :]
        spread = jnp.broadcast_to(diag, (BLOCK, 4 * BLOCK))
        tile = pltpu.roll(spread, 0, 1, stride=1, stride_axis=0)[:, BLOCK:].T
        low_far = jnp.broadcast_to(diag[:, 1:2], (BLOCK, BLOCK))
        high_far = jnp.broadcast_to(diag[:, 4 * BLOCK - 1 :], (BLOCK, BLOCK))
        bias_tiles.append((low_far, tile, high_far))
    turned_vals = vals.astype(f32).T.astype(bf16)
    upper = lax.broadcasted_iota(i32, (BLOCK, 1), 0) < half
    for i in range(blocks):
        rows = slice(i * BLOCK, (i + 1) * BLOCK)
        same = cols_ref[:, seg_line : seg_line + 1] == row_ids[:, rows]
        queries = q_ref[rows, :]
        outs = []
        for s in range(2):
            mask = jnp.where(lane // half == s, scale, 0.0).astype(bf16)
            scores = mm(keys, queries * mask, NT)
            low_far, tile, high_far = bias_tiles[s]
            pieces = []
            for j in range(blocks):
                if j - i < -1:
                    pieces.append(low_far)
                elif j - i > 1:
                    pieces.append(high_far)
                else:
                    start = (j - i + 1) * BLOCK
                    pieces.append(tile[start : start + BLOCK])
            scores = scores + jnp.concatenate(pieces, axis=0)
            scores = jnp.where(same, scores, -1000000000.0)
            top = jnp.max(scores, axis=0, keepdims=True)
            grown = jnp.exp(scores - top)
            probs = (grown * (1.0 / jnp.sum(grown, axis=0, keepdims=True))).astype(bf16)
            probs_ref[s, :, rows] = probs
            outs.append(mm(turned_vals, probs))
        att_ref[rows, :] = jnp.where(upper, outs[0], outs[1]).T.astype(bf16)


def chosen_of(router, cols_ref, line):
    pick = cols_ref[:, line : line + 1] == lane_numbers(*router.shape)
    return pick, jnp.sum(jnp.where(pick, router, 0.0), axis=-1, keepdims=True)


def route_kernel(tok_ref, att_a_ref, att_b_ref, w_out_ref, gain_ref, w_router_ref, rows_ref, residual_ref, router_ref, sent_ref):
    near = att_a_ref.shape[1]
    branch = mm(att_a_ref[...], w_out_ref[:near]) + mm(att_b_ref[...], w_out_ref[near:])
    residual = tok_ref[...].astype(f32) + branch
    residual_ref[...] = residual
    inverse = lax.rsqrt(jnp.mean(residual * residual, axis=-1, keepdims=True) + eps)
    normed = residual * inverse * gain_ref[...]
    low = normed.astype(bf16)
    tokens = low.shape[0]
    direct = len(sent_ref.shape) == 4
    local_experts = sent_ref.shape[1] if direct else sent_ref.shape[0]
    slots = sent_ref.shape[0] * sent_ref.shape[2] if direct else sent_ref.shape[1]
    for index in range(local_experts):
        table = lax.broadcasted_iota(i32, (slots, tokens), 0) == rows_ref[index : index + 1, :]
        rows = mm(one_hot(table), low)
        if direct:
            by_group(rows, sent_ref, index)
        else:
            sent_ref[index] = rows.astype(bf16)
    w_high, w_low = split(w_router_ref[...])
    low_rest = (normed - low.astype(f32)).astype(bf16)
    experts = w_high.shape[1]
    logits = mm(low, jnp.concatenate([w_high, w_low], axis=1))
    logits = logits[:, :experts] + logits[:, experts:] + mm(low_rest, w_high)
    top = jnp.max(logits, axis=-1, keepdims=True)
    grown = jnp.exp(logits - top)
    router = grown / jnp.sum(grown, axis=-1, keepdims=True)
    router_ref[...] = router


def expert_kernel(place_ref, x_ref, cot_ref, w_in_ref, w_back_ref, *refs, parts, le, groups, order, olds):
    count = len(order)
    refs = refs[olds:]
    back_refs = refs[:count]
    act_ref, gp_ref = refs[count : count + 2]
    x_buf, g_buf, w_in_buf, w_back_buf, act_buf, gp_buf, back_buf = refs[count + 2 : -4]
    x_sem, g_sem, w_sem, put_sem = refs[-4:]
    place = place_ref[0]
    whole = [(place + j) % parts for j in order]
    load_in = pltpu.make_async_copy(w_in_ref.at[le], w_in_buf, w_sem.at[0])
    load_back = pltpu.make_async_copy(w_back_ref.at[le], w_back_buf, w_sem.at[1])
    load_in.start()
    loads = []
    for at in range(count):
        loads.append(
            (
                pltpu.make_async_copy(x_ref.at[whole[at]], x_buf.at[at], x_sem.at[at]),
                pltpu.make_async_copy(cot_ref.at[whole[at]], g_buf.at[at], g_sem.at[at]),
            )
        )
        loads[at][0].start()
    load_back.start()
    for at in range(count):
        loads[at][1].start()
    load_in.wait()
    scale = (2.0 / jnp.pi) ** 0.5
    slots, model = x_buf.shape[1:]
    hidden = act_buf.shape[2]
    spare = back_buf.shape[1] - slots
    line = lax.broadcasted_iota(i32, (spare, BLOCK), 0)
    capacity = slots // groups
    puts = []

    def put(source, target, kind, at):
        copy = pltpu.make_async_copy(source, target, put_sem.at[kind, at])
        copy.start()
        puts.append(copy)

    span = 2
    for first in range(0, count, span):
        ats = range(first, first + span)
        for at in ats:
            loads[at][0].wait()
        pre = mm(x_buf[first : first + span].reshape(span * slots, model), w_in_buf[...])
        for at in ats:
            loads[at][1].wait()
        if first == 0:
            load_back.wait()
        grad = mm(g_buf[first : first + span].reshape(span * slots, model), w_back_buf[...], NT)
        square = pre * pre
        slant = jnp.tanh(scale * pre * (1.0 + 0.044715 * square))
        act = (0.5 * pre * (1.0 + slant)).astype(bf16)
        act_buf[first : first + span] = act.reshape(span, slots, hidden)
        slope = 0.5 * (1.0 + slant) + 0.5 * pre * (1.0 - slant * slant) * (
            scale * (1.0 + 3.0 * 0.044715 * square)
        )
        gp = (grad * slope).astype(bf16)
        gp_buf[first : first + span] = gp.reshape(span, slots, hidden)
        back = mm(gp, w_in_buf[...], NT).astype(bf16)
        back_buf[first : first + span, :slots] = back.reshape(span, slots, model)
        all_dots = jnp.sum(act.astype(f32) * grad, axis=-1, keepdims=True)
        for at in ats:
            put(act_buf.at[at], act_ref.at[whole[at]], 0, at)
            put(gp_buf.at[at], gp_ref.at[whole[at]], 1, at)
            dots = all_dots[(at - first) * slots : (at - first + 1) * slots]
            dots = jnp.broadcast_to(dots, (slots, BLOCK)).T
            laid = jnp.zeros((spare, BLOCK), f32)
            for group in range(groups):
                piece = dots[:1, group * capacity : (group + 1) * capacity]
                piece = jnp.concatenate([piece, jnp.zeros((1, BLOCK - capacity), f32)], axis=1)
                laid = jnp.where(line == group, piece, laid)
            back_buf[at, slots:] = jnp.zeros((spare, model), bf16)
            back_buf[at, slots:, :BLOCK] = laid.astype(bf16)
            put(back_buf.at[at], back_refs[at], 2, at)
    for copy in puts:
        copy.wait()


def expert_weights_kernel(own_ref, x_ref, cot_ref, gp_ref, w_router_ref, all_act_ref, w_back_ref, *refs, le, local_experts):
    in_ref, back_ref, out_ref, gs_ref, gate_ref, turned_ref = refs[-6:]
    parts = x_ref.shape[0]

    def flat(values):
        return values.reshape(-1, values.shape[-1])

    @pl.when(pl.program_id(0) == 0)
    def _():
        w_high, w_low = split(w_router_ref[...])
        number = own_ref[0] * local_experts + le
        for part in range(parts):
            rows = x_ref[part]
            logits = mm(rows, w_high) + mm(rows, w_low)
            grown = jnp.exp(logits - jnp.max(logits, axis=-1, keepdims=True))
            pick = lane_numbers(*logits.shape) == number
            gate = jnp.sum(jnp.where(pick, grown, 0.0), axis=-1, keepdims=True)
            gate = gate / jnp.sum(grown, axis=-1, keepdims=True)
            gate_ref[part] = gate
            gs_ref[part] = (cot_ref[part].astype(f32) * gate).astype(bf16)
        turned_ref[...] = flat(x_ref[...]).T

    gp = (gp_ref[...].astype(f32) * gate_ref[...]).astype(bf16)
    in_ref[0] = mm(turned_ref[...], flat(gp))
    third = back_ref.shape[1]
    begin = pl.multiple_of(pl.program_id(0) * third, third)
    back_ref[0] = mm(flat(all_act_ref[:, :, pl.ds(begin, third)]), flat(gs_ref[...]), TN)
    out = mm(flat(all_act_ref[...]), w_back_ref[0])
    slots = out.shape[0] // parts
    for part in range(parts):
        rows = out[part * slots : (part + 1) * slots]
        if len(out_ref.shape) == 5:
            by_group(rows, out_ref.at[part], 0)
        else:
            out_ref[part, 0] = rows.astype(bf16)


def middle_kernel(residual_ref, cot_ref, gain_ref, w_router_ref, router_ref, cols_ref, w_out_ref, *refs, capacity, stride):
    grad_res_ref, branch_ref, att_ref, extra_ref = refs[-4:]
    back_refs = refs[:-4]
    local_experts = len(back_refs)
    tokens = residual_ref.shape[0]
    rows = None
    grad_gate = None
    for index, back_ref in enumerate(back_refs):
        key = cols_ref[:, index : index + 1]
        group = key // capacity
        number = lane_numbers(tokens, back_ref.shape[0])
        back = back_ref[...]
        part = mm(one_hot(number == key + group * (stride - capacity)), back)
        lines = mm(one_hot(number == group * stride + capacity), back[:, :BLOCK])
        slot = lane_numbers(tokens, BLOCK) == key - group * capacity
        picked = jnp.sum(jnp.where(slot, lines, 0.0), axis=-1, keepdims=True)
        rows = part if rows is None else rows + part
        grad_gate = picked if grad_gate is None else grad_gate + picked
    router = router_ref[...]
    pick, chosen = chosen_of(router, cols_ref, local_experts)
    grad_logits = router * (pick.astype(f32) - chosen) * grad_gate
    residual = residual_ref[...]
    inverse = lax.rsqrt(jnp.mean(residual * residual, axis=-1, keepdims=True) + eps)
    gain = gain_ref[...]
    scaled = residual * inverse
    logits_high, logits_low = split(grad_logits)
    w_high, w_low = split(w_router_ref[...])
    grad_normed = chosen * rows + mm(
        jnp.concatenate([logits_high, logits_low, logits_high], axis=1),
        jnp.concatenate([w_high, w_high, w_low], axis=1),
        NT,
    )
    weighted = grad_normed * gain
    lean = jnp.mean(weighted * residual, axis=-1, keepdims=True)
    grad_res = cot_ref[...].astype(f32) + (
        inverse * weighted - residual * (inverse * inverse * inverse) * lean
    )
    grad_res_ref[...] = grad_res
    low = grad_res.astype(bf16)
    branch_ref[...] = low
    att_ref[...] = mm(low, w_out_ref[...], NT).astype(bf16)
    gain_grad = jnp.sum(grad_normed * scaled, axis=0, keepdims=True)
    normed_high, normed_low = split(scaled * gain)
    experts = logits_high.shape[1]
    router_grad = mm(jnp.concatenate([logits_high, logits_low], axis=1), normed_high, TN)
    router_grad = router_grad[:experts] + router_grad[experts:] + mm(logits_high, normed_low, TN)
    spare = extra_ref.shape[1] - router_grad.shape[0] - 1
    both = jnp.concatenate(
        [router_grad, gain_grad, jnp.zeros((spare, gain_grad.shape[1]), f32)], axis=0
    )
    extra_ref[...] = both.T.astype(bf16)


def attend_back_kernel(q_ref, k_ref, v_ref, probs_ref, grad_ref, turned_ref, *refs, kind, head_start, buckets):
    if kind == 0:
        att_a_ref, att_b_ref, branch_ref, extra_ref = refs[:4]
    else:
        old_diag_ref = refs[0]
    if kind == 2:
        old_weight_ref = refs[1]
    dq_ref, dk_ref, dv_ref, weight_ref, diag_ref, slope_ref = refs[-6:]
    step = pl.program_id(0)
    length = k_ref.shape[0]
    blocks = length // BLOCK
    lane = lane_numbers(1, BLOCK)
    half = BLOCK // 2
    scale = half**-0.5
    keys = k_ref[...]
    vals = v_ref[...]
    queries = q_ref[...]
    grads = grad_ref[...]
    static_columns = weight_ref.shape[1]

    @pl.when(step == 0)
    def _():
        if kind == 0:
            diag_ref[...] = jnp.zeros_like(diag_ref)
            model = branch_ref.shape[1]
            tail = extra_ref.shape[1]
            begin = static_columns - tail - model
            near = att_a_ref.shape[1]
            branch = branch_ref[...]
            weight_ref[:near, begin : begin + model] = mm(att_a_ref[...], branch, TN).astype(bf16)
            weight_ref[near:, begin : begin + model] = mm(att_b_ref[...], branch, TN).astype(bf16)
            weight_ref[:, begin + model :] = extra_ref[...]
        else:
            diag_ref[...] = old_diag_ref[...]
        if kind == 2:
            weight_ref[:, : old_weight_ref.shape[1]] = old_weight_ref[...]

    across = lax.broadcasted_iota(i32, (BLOCK, BLOCK), 0) + lane_numbers(BLOCK, BLOCK)
    flip = one_hot(across == BLOCK - 1)
    turned_keys = keys.astype(f32).T.astype(bf16)
    dq = [[] for _ in range(blocks)]
    dk, dv = [], []
    for s in range(2):
        mask = jnp.where(lane // half == s, 1.0, 0.0).astype(bf16)
        near = [None, None, None]
        far = [None, None]
        for i in range(blocks):
            rows = slice(i * BLOCK, (i + 1) * BLOCK)
            probs = probs_ref[s, :, rows].astype(f32)
            grad_probs = mm(vals, grads[rows] * mask, NT)
            delta = jnp.sum(probs * grad_probs, axis=0, keepdims=True)
            slope = probs * (grad_probs - delta)
            low = slope.astype(bf16)
            slope_ref[s, :, rows] = low
            dq[i].append(mm(turned_keys, low))
            for j in range(blocks):
                piece = slope[j * BLOCK : (j + 1) * BLOCK]
                apart = j - i
                if abs(apart) <= 1:
                    old = near[1 - apart]
                    near[1 - apart] = piece if old is None else old + piece
                else:
                    old = far[int(apart > 0)]
                    far[int(apart > 0)] = piece if old is None else old + piece
        dk.append(mm(slope_ref[s], queries))
        dv.append(mm(probs_ref[s], grads))
        wide = jnp.concatenate([jnp.zeros_like(near[0])] + near, axis=1)
        lined = pltpu.roll(mm(flip, wide.astype(bf16)), 3 * BLOCK + 1, 1, stride=1, stride_axis=0)
        lined = jnp.concatenate([lined, far[0], far[1]], axis=1)
        diag_ref[pl.ds(head_start + 2 * step + s, 1), :] = jnp.sum(lined, axis=0, keepdims=True)
    upper = lax.broadcasted_iota(i32, (BLOCK, 1), 0) < half
    dq_low = jnp.concatenate([jnp.where(upper, *item).T for item in dq], axis=0)
    dq_low = (dq_low * scale).astype(bf16)
    left = lane < half
    dk_low = (jnp.where(left, dk[0], dk[1]) * scale).astype(bf16)
    dv_low = jnp.where(left, dv[0], dv[1]).astype(bf16)
    dq_ref[...] = dq_low
    dk_ref[...] = dk_low
    dv_ref[...] = dv_low
    begin = 0 if kind < 2 else old_weight_ref.shape[1]
    begin = pl.multiple_of(step * (3 * BLOCK) + begin, 3 * BLOCK)
    weight_ref[:, pl.ds(begin, 3 * BLOCK)] = mm(
        turned_ref[...], jnp.concatenate([dq_low, dk_low, dv_low], axis=1)
    ).astype(bf16)
    if kind == 2:

        @pl.when(step == pl.num_programs(0) - 1)
        def _():
            wide = diag_ref.shape[1]
            number = lane_numbers(buckets, wide)
            bucket = bucket_of(2 * BLOCK - number)
            bucket = jnp.where(number >= 4 * BLOCK, 15, bucket)
            bucket = jnp.where(number >= 5 * BLOCK, 31, bucket)
            pick = bucket == lax.broadcasted_iota(i32, (buckets, wide), 0)
            rows = jnp.concatenate(
                [diag_ref[...], jnp.zeros((BLOCK - diag_ref.shape[0], wide), f32)], axis=0
            )
            bias = mm_exact(pick.astype(f32), rows, NT)
            begin = static_columns - BLOCK
            weight_ref[:, begin:] = jnp.zeros((weight_ref.shape[0], BLOCK), bf16)
            weight_ref[:buckets, begin:] = bias.astype(bf16)


def tokens_kernel(tok_ref, gain_ref, w_ref, grad_res_ref, *refs):
    out_ref = refs[-1]
    parts = refs[:-1]
    groups = len(parts) // 3
    model = tok_ref.shape[1]
    grad_normed = None
    for part in range(3):
        start = part * model
        for group in range(groups):
            block = parts[3 * group + part]
            width = block.shape[1]
            piece = mm(block[...], w_ref[:, start : start + width], NT)
            grad_normed = piece if grad_normed is None else grad_normed + piece
            start += width
    values = tok_ref[...].astype(f32)
    inverse = lax.rsqrt(jnp.mean(values * values, axis=-1, keepdims=True) + eps)
    weighted = grad_normed * gain_ref[...]
    lean = jnp.mean(weighted * values, axis=-1, keepdims=True)
    out_ref[...] = grad_res_ref[...] + (
        inverse * weighted - values * (inverse * inverse * inverse) * lean
    )


def output_kernel(residual_ref, router_ref, cols_ref, rows_ref, out_ref):
    tokens = residual_ref.shape[0]
    local_experts, slots = rows_ref.shape[:2]
    mixture = None
    for index in range(local_experts):
        turned = cols_ref[:, index : index + 1] == lane_numbers(tokens, slots)
        part = mm(one_hot(turned), rows_ref[index])
        mixture = part if mixture is None else mixture + part
    _, chosen = chosen_of(router_ref[...], cols_ref, local_experts)
    out_ref[...] = (residual_ref[...] + chosen * mixture).astype(bf16)


def finish_kernel(where_ref, a_ref, b_ref, w_ref, *refs):
    qkv_ref, out_ref, gain_ref, extra_ref = refs[-4:]
    place = where_ref[2]
    parts = a_ref.shape[1]
    model = out_ref.shape[3]
    pairs = model // BLOCK
    near = pairs // 3
    for k in range(parts):
        z = (place + parts - k) % parts
        a = a_ref[0, k].astype(f32)
        b = b_ref[0, k].astype(f32)
        total = None
        for part in range(3):
            pieces = [
                (a if p < near else b)[:, ((p if p < near else p - near) * 3 + part) * BLOCK :][
                    :, :BLOCK
                ]
                for p in range(pairs)
            ]
            whole = jnp.concatenate(pieces, axis=1)
            span = slice(part * model, (part + 1) * model)
            qkv_ref[0, z, :, span] = whole
            w = w_ref[0, z, :, span].astype(f32)
            share = jnp.sum(whole * w, axis=-1, keepdims=True)
            total = share if total is None else total + share
        gain_ref[0, z] = jnp.broadcast_to(total, gain_ref.shape[2:])
        begin = near * 3 * BLOCK
        out_ref[0, z] = a[:, begin : begin + model]
        tail = a.shape[1] - begin - model
        extra_ref[0, z, :, :tail] = a[:, begin + model :]
        extra_ref[0, z, :, tail:] = b[:, (pairs - near) * 3 * BLOCK :]


def small_kernel(gain_ref, sums_ref, extra_ref, router_ref, gains_ref, bias_ref, *, experts, at):
    extras = extra_ref[:, :at].T
    router_ref[...] = extras[:experts]
    gains_ref[0:1, :] = sums_ref[...].T[0:1] / gain_ref[...]
    gains_ref[1:2, :] = extras[experts : experts + 1]
    heads, buckets = bias_ref.shape
    bias_ref[...] = extra_ref[:BLOCK, at:].T[:heads, :buckets]


def add_low(left, right):
    return (left.astype(f32) + right.astype(f32)).astype(bf16)


def tie(items, after):
    return lax.optimization_barrier((items, after))[0]


def held(kernel, start, after):
    def body(*refs):
        kernel(*refs[:start], *refs[start + len(after) :])

    return body


class Scatter:
    def __init__(self, blocks):
        self.parts = lax.axis_size("hidden")
        self.blocks = blocks
        self.count = 0

    def step(self, after=()):
        self.count += 1
        right, left = self.blocks[self.parts - self.count], self.blocks[self.count]
        if self.count > 1:
            right, left = add_low(right, self.right), add_low(left, self.left)
        right, left = tie((right, left), after)
        ways = [(a, a + 1) for a in range(self.count)]
        self.right = lax.ppermute(right, "hidden", ways)
        ways = [(a, a - 1) for a in range(self.parts - self.count, self.parts)]
        self.left = lax.ppermute(left, "hidden", ways)

    def last(self):
        return self.right, self.left

    def finish(self, after=()):
        right, left = tie(self.last(), after)
        total = self.blocks[0].astype(f32) + right.astype(f32) + left.astype(f32)
        return total.astype(bf16)


def pick_block(blocks, index):
    return lax.dynamic_index_in_dim(blocks, index, 0, keepdims=False)


class Sum:
    def __init__(self, values):
        self.groups = lax.axis_size("expert")
        self.parts = lax.axis_size("hidden")
        self.own = lax.axis_index("expert")
        self.place = lax.axis_index("hidden")
        self.core = self.own % 2
        self.chip = self.own // 2
        self.chips = self.groups // 2
        self.pair = [(a, a ^ 1) for a in range(self.groups)]
        self.width = values.shape[1]
        self.values = values

    def cores(self):
        halves = self.values.reshape(2, -1, self.width)
        got = lax.ppermute(pick_block(halves, 1 - self.core), "expert", self.pair)
        self.values = add_low(pick_block(halves, self.core), got)

    def cores_at_once(self):
        teams = [[2 * a, 2 * a + 1] for a in range(self.chips)]
        got = lax.all_to_all(
            self.values, "expert", split_axis=0, concat_axis=0, tiled=True, axis_index_groups=teams
        ).reshape(2, -1, self.width)
        self.values = add_low(got[0], got[1])

    def plane(self):
        pieces = self.values.reshape(self.chips, -1, self.width)
        total = pick_block(pieces, self.chip).astype(f32)
        for step in range(1, self.chips):
            ways = [(a, a ^ (2 * step)) for a in range(self.groups)]
            got = lax.ppermute(pick_block(pieces, self.chip ^ step), "expert", ways)
            total = total + got.astype(f32)
        self.values = total.astype(bf16)

    def line(self):
        pieces = self.values.reshape(self.parts, -1, self.width)
        total = pick_block(pieces, self.place).astype(f32)
        for step in range(1, self.parts):
            ways = [(a, (a + step) % self.parts) for a in range(self.parts)]
            got = lax.ppermute(pick_block(pieces, (self.place + step) % self.parts), "hidden", ways)
            total = total + got.astype(f32)
        self.values = total.astype(bf16)

    def line_back(self):
        pieces = [self.values]
        for step in range(1, self.parts):
            ways = [(a, (a + step) % self.parts) for a in range(self.parts)]
            pieces.append(lax.ppermute(self.values, "hidden", ways))
        self.values = jnp.stack(pieces)

    def plane_back(self):
        pieces = [self.values]
        for step in range(1, self.chips):
            ways = [(a, a ^ (2 * step)) for a in range(self.groups)]
            pieces.append(lax.ppermute(self.values, "expert", ways))
        self.values = jnp.stack(pieces)

    def cores_back(self):
        return self.values, lax.ppermute(self.values, "expert", self.pair)

    def run(self):
        self.cores()
        self.plane()
        self.line()
        self.line_back()
        self.plane_back()
        return self.cores_back()


def local(tokens, cotangent, segments, routes, slot_ids, kept_flags, gain_one, w_qkv, w_out, bias_table, gain_two, w_router, w_in, w_back):
    tok_rows, model = tokens.shape
    bucket_count, head_count = bias_table.shape
    experts = w_router.shape[1]
    local_experts = w_in.shape[0]
    hidden = w_in.shape[2]
    groups = lax.axis_size("expert")
    parts = lax.axis_size("hidden")
    own = lax.axis_index("expert")
    place = lax.axis_index("hidden")
    capacity = max(2, (5 * tok_rows + 4 * experts - 1) // (4 * experts))
    slots = groups * capacity
    pairs = head_count // 2
    shape = jax.ShapeDtypeStruct
    vmem = pl.BlockSpec(memory_space=pltpu.VMEM)
    any_space = pl.BlockSpec(memory_space=pl.ANY)
    gain_one_row = gain_one[None, :]
    gain_two_row = gain_two[None, :]
    seg_line = local_experts + 1

    def exchange(rows, axis=0):
        return lax.all_to_all(rows, "expert", split_axis=axis, concat_axis=axis, tiled=True)

    cot_near = lax.all_gather(cotangent, "hidden", axis=0, tiled=False)
    id_rows, id_cols, diag_bias = pl.pallas_call(
        functools.partial(place_kernel, capacity=capacity, local_experts=local_experts),
        out_shape=[
            shape((8, tok_rows), i32),
            shape((tok_rows, BLOCK), i32),
            shape((head_count, 4 * BLOCK), f32),
        ],
        in_specs=[vmem] * 5,
        out_specs=[vmem] * 3,
        compiler_params=params(),
        cost_estimate=cost(1e8, 1e6),
        name="place",
    )(routes[None, :], slot_ids[None, :], kept_flags[None, :], segments, bias_table)
    qkv, turned = pl.pallas_call(
        qkv_kernel,
        grid=(3,),
        out_shape=[shape((tok_rows, 3 * model), bf16), shape((model, tok_rows), bf16)],
        in_specs=[
            pl.BlockSpec((tok_rows, model), lambda j: (0, 0)),
            pl.BlockSpec((1, model), lambda j: (0, 0)),
            pl.BlockSpec((model, model), lambda j: (0, j)),
        ],
        out_specs=[
            pl.BlockSpec((tok_rows, model), lambda j: (0, j)),
            pl.BlockSpec((model, tok_rows), lambda j: (0, 0)),
        ],
        scratch_shapes=[pltpu.VMEM((tok_rows, model), bf16)],
        compiler_params=params(("arbitrary",)),
        cost_estimate=cost(6 * tok_rows * model * model, 8 * model * model * 2),
        name="qkv",
    )(tokens, gain_one_row, w_qkv)

    def pair_spec(offset):
        return pl.BlockSpec((tok_rows, BLOCK), lambda p: (0, offset + p))

    steps = pairs // 2
    attended, probs = [], []
    for half in range(2):
        start = half * steps
        att, prob = pl.pallas_call(
            functools.partial(attend_kernel, seg_line=seg_line, head_start=2 * start),
            grid=(steps,),
            out_shape=[
                shape((tok_rows, steps * BLOCK), bf16),
                shape((2 * steps, tok_rows, tok_rows), bf16),
            ],
            in_specs=[
                pair_spec(start),
                pair_spec(pairs + start),
                pair_spec(2 * pairs + start),
                pl.BlockSpec((8, tok_rows), lambda p: (0, 0)),
                pl.BlockSpec((tok_rows, BLOCK), lambda p: (0, 0)),
                pl.BlockSpec((head_count, 4 * BLOCK), lambda p: (0, 0)),
            ],
            out_specs=[
                pair_spec(0),
                pl.BlockSpec((2, tok_rows, tok_rows), lambda p: (p, 0, 0)),
            ],
            compiler_params=params(("arbitrary",)),
            cost_estimate=cost(steps * 4e9, steps * 3e6),
            name="attend",
        )(qkv, qkv, qkv, id_rows, id_cols, diag_bias)
        attended.append(att)
        probs.append(prob)

    def by_slots(count):
        if direct:
            return shape((groups, count, capacity, model), bf16)
        return shape((count, slots, model), bf16)

    direct = capacity % 8 == 0
    residual, router, sent_rows = pl.pallas_call(
        route_kernel,
        out_shape=[
            shape((tok_rows, model), f32),
            shape((tok_rows, experts), f32),
            by_slots(local_experts),
        ],
        in_specs=[vmem] * 7,
        out_specs=[vmem] * 3,
        compiler_params=params(),
        cost_estimate=cost(6e9, 6e6),
        name="route",
    )(tokens, *attended, w_out, gain_two_row, w_router, id_rows)

    place_arr = place.astype(i32).reshape(1)
    own_arr = own.astype(i32).reshape(1)
    spare = -(-groups // 16) * 16
    block = shape((slots + spare, model), bf16)
    stack = shape((parts, slots, hidden), bf16)
    smem = pl.BlockSpec(memory_space=pltpu.SMEM)
    third = hidden // 3

    def run_experts(le, order, olds, after=()):
        count = len(order)
        results = pl.pallas_call(
            held(
                functools.partial(
                    expert_kernel, parts=parts, le=le, groups=groups, order=order, olds=len(olds)
                ),
                5 + len(olds),
                after,
            ),
            out_shape=[block] * count + [stack, stack],
            in_specs=[smem] + [any_space] * (4 + len(olds) + len(after)),
            out_specs=[any_space] * (count + 2),
            input_output_aliases={5 + n: count + n for n in range(len(olds))},
            scratch_shapes=[
                pltpu.VMEM((count, slots, model), bf16),
                pltpu.VMEM((count, slots, model), bf16),
                pltpu.VMEM((model, hidden), bf16),
                pltpu.VMEM((hidden, model), bf16),
                pltpu.VMEM((count, slots, hidden), bf16),
                pltpu.VMEM((count, slots, hidden), bf16),
                pltpu.VMEM((count, slots + spare, model), bf16),
                pltpu.SemaphoreType.DMA((count,)),
                pltpu.SemaphoreType.DMA((count,)),
                pltpu.SemaphoreType.DMA((2,)),
                pltpu.SemaphoreType.DMA((3, count)),
            ],
            compiler_params=params(),
            cost_estimate=cost(4 * count * slots * model * hidden, 1e7),
            name="experts",
        )(place_arr, rows_all[le], cot_all[le], w_in, w_back, *olds, *after)
        return results[:count], list(results[count:])

    def run_both(le, after=()):
        ends = list(range(1, parts, 2))
        rest = list(range(0, parts, 2))
        backs = [None] * parts
        some, kept = run_experts(le, ends, [], after)
        for j, item in zip(ends, some):
            backs[j] = item
        some, kept = run_experts(le, rest, kept)
        for j, item in zip(rest, some):
            backs[j] = item
        return backs, kept

    def run_weights(le, kept, olds, after):
        act, gp = kept
        stack_spec = pl.BlockSpec((parts, slots, model), lambda j: (0, 0, 0))
        hidden_spec = pl.BlockSpec((parts, slots, third), lambda j: (0, 0, j))
        return pl.pallas_call(
            held(
                functools.partial(expert_weights_kernel, le=le, local_experts=local_experts),
                7 + len(olds),
                after,
            ),
            grid=(3,),
            out_shape=[
                shape((local_experts, model, hidden), f32),
                shape((local_experts, hidden, model), f32),
                shape((parts,) + by_slots(local_experts).shape, bf16),
            ],
            in_specs=[
                smem,
                stack_spec,
                stack_spec,
                hidden_spec,
                pl.BlockSpec((model, experts), lambda j: (0, 0)),
                pl.BlockSpec((parts, slots, hidden), lambda j: (0, 0, 0)),
                pl.BlockSpec((1, hidden, model // 3), lambda j: (le, 0, j)),
            ]
            + [any_space] * (len(olds) + len(after)),
            out_specs=[
                pl.BlockSpec((1, model, third), lambda j: (le, 0, j)),
                pl.BlockSpec((1, third, model), lambda j: (le, j, 0)),
                pl.BlockSpec(
                    (parts, groups, 1, capacity, model // 3), lambda j: (0, 0, le, 0, j)
                )
                if direct
                else pl.BlockSpec((parts, 1, slots, model // 3), lambda j: (0, le, 0, j)),
            ],
            scratch_shapes=[
                pltpu.VMEM((parts, slots, model), bf16),
                pltpu.VMEM((parts, slots, 1), f32),
                pltpu.VMEM((model, parts * slots), bf16),
            ],
            input_output_aliases={7 + n: n for n in range(len(olds))},
            compiler_params=params(("arbitrary",)),
            cost_estimate=cost(4 * parts * slots * model * hidden, 1.3e7),
            name="expert_weights",
        )(own_arr, rows_all[le], cot_all[le], gp, w_router, act, w_back, *olds, *after)

    def own_slots(le, ids, after):
        return pl.pallas_call(
            held(functools.partial(slots_kernel, parts=parts, le=le), 2 + parts, after),
            out_shape=by_slots(parts),
            in_specs=[smem] + [vmem] * (parts + 1) + [any_space] * len(after),
            out_specs=vmem,
            compiler_params=params(),
            cost_estimate=cost(2e9, 6e6),
            name="slots",
        )(place_arr, *ids, cot_near, *after)

    def exchange_slots(rows):
        if not direct:
            return exchange(rows, 1)
        return exchange(rows).transpose(1, 0, 2, 3).reshape(-1, slots, model)

    here = exchange_slots(sent_rows)
    rows_all = [
        lax.all_gather(here[le], "hidden", axis=0, tiled=False) for le in range(local_experts)
    ]
    ids = [id_rows]
    far_ids = tie(id_rows, here)
    for step in range(1, parts):
        ways = [((a + step) % parts, a) for a in range(parts)]
        ids.append(lax.ppermute(far_ids, "hidden", ways))
    cot_slots = [own_slots(0, ids, [here])]
    cot_slots.append(own_slots(1, ids, cot_slots))
    cot_all = [exchange_slots(cot_slots[0])]
    cot_all.append(exchange_slots(tie(cot_slots[1], cot_all[0])))
    backs, kept = run_both(0, cot_slots[1:])
    sum_first = Scatter(backs)
    sum_first.step()
    grads = run_weights(0, kept, [], [])
    sum_first.step(grads)
    backs, kept_second = run_both(1, grads[:1])
    sum_second = Scatter(backs)
    sum_second.step()
    sum_second.step(sum_first.last())
    sum_first.step()
    grads = run_weights(1, kept_second, grads, sum_second.last()[:1])

    def with_dots(total):
        rows = total[:slots].reshape(groups, capacity, model)
        dots = total[slots : slots + groups].reshape(groups, 1, model)
        dots = jnp.pad(dots, ((0, 0), (0, stride - capacity - 1), (0, 0)))
        return jnp.concatenate([rows, dots], axis=1).reshape(groups * stride, model)

    stride = -(-(capacity + 1) // 8) * 8
    back_first = exchange(with_dots(sum_first.finish()))
    sum_second.step(sum_first.last())
    back_second = sum_second.finish((back_first, grads))
    backs = [back_first, exchange(with_dots(back_second))]
    grad_w_in, grad_w_back, out_sums = grads
    extra_width = -(-(experts + 1) // BLOCK) * BLOCK

    grad_res, grad_branch, grad_att, extra = pl.pallas_call(
        functools.partial(middle_kernel, capacity=capacity, stride=stride),
        out_shape=[
            shape((tok_rows, model), f32),
            shape((tok_rows, model), bf16),
            shape((tok_rows, model), bf16),
            shape((model, extra_width), bf16),
        ],
        in_specs=[vmem] * (7 + local_experts),
        out_specs=[vmem] * 4,
        compiler_params=params(),
        cost_estimate=cost(6e9, 8e6),
        name="middle",
    )(residual, cotangent, gain_two_row, w_router, router, id_cols, w_out, *backs)

    out_rows = lax.psum_scatter(out_sums, "hidden", scatter_dimension=0, tiled=False)
    out_ready = out_rows
    out_rows = exchange_slots(out_rows)
    output = pl.pallas_call(
        output_kernel,
        out_shape=shape((tok_rows, model), bf16),
        in_specs=[vmem] * 4,
        out_specs=vmem,
        compiler_params=params(),
        cost_estimate=cost(1e9, 4e6),
        name="output",
    )(residual, router, id_cols, out_rows)

    def run_back(kind, start, count, extras, width):
        inner = start % steps
        return pl.pallas_call(
            functools.partial(
                attend_back_kernel,
                kind=kind,
                head_start=2 * start,
                buckets=bucket_count,
            ),
            grid=(count,),
            out_shape=[shape((tok_rows, count * BLOCK), bf16)] * 3
            + [shape((model, width), bf16), shape((16, 6 * BLOCK), f32)],
            in_specs=[
                pair_spec(start),
                pair_spec(pairs + start),
                pair_spec(2 * pairs + start),
                pl.BlockSpec((2, tok_rows, tok_rows), lambda p: (inner + p, 0, 0)),
                pair_spec(start),
                pl.BlockSpec((model, tok_rows), lambda p: (0, 0)),
            ]
            + [pl.BlockSpec(item.shape, lambda p: (0, 0)) for item in extras],
            out_specs=[pair_spec(0)] * 3
            + [
                pl.BlockSpec((model, width), lambda p: (0, 0)),
                pl.BlockSpec((16, 6 * BLOCK), lambda p: (0, 0)),
            ],
            scratch_shapes=[pltpu.VMEM((2, tok_rows, tok_rows), bf16)],
            compiler_params=params(("arbitrary",)),
            cost_estimate=cost(count * 4e9, count * 3e6),
            name="attend_back",
        )(qkv, qkv, qkv, probs[start // steps], grad_att, turned, *extras)

    wide = 3 * BLOCK
    early = pairs // 3
    first = run_back(
        0, 0, early, [*attended, grad_branch, extra], wide * early + model + extra_width
    )
    sum_a = Sum(first[3])
    sum_a.cores()
    second = run_back(1, early, 1, [first[4]], wide)
    sum_a.values = tie(sum_a.values, second[3])
    sum_a.plane()
    third_part = run_back(
        2, early + 1, pairs - early - 1, [second[4], second[3]], wide * (pairs - early) + BLOCK
    )
    sum_b = Sum(tie(third_part[3], sum_a.values))
    sum_b.cores()
    grad_parts = [*first[:3], *second[:3], *third_part[:3]]
    grad_tokens = pl.pallas_call(
        held(tokens_kernel, 4 + len(grad_parts), [sum_b.values]),
        out_shape=shape((tok_rows, model), f32),
        in_specs=[vmem] * (4 + len(grad_parts)) + [any_space],
        out_specs=vmem,
        compiler_params=params(),
        cost_estimate=cost(3e9, 1e7),
        name="tokens_grad",
    )(tokens, gain_one_row, w_qkv, grad_res, *grad_parts, sum_b.values)
    sum_a.line()
    sum_b.plane()
    sum_a.line_back()
    sum_b.line()
    sum_a.plane_back()
    sum_b.line_back()
    sum_b.values = tie(sum_b.values, (out_rows, grad_tokens))
    sums = [sum_a.cores_back()]
    sum_b.plane_back()
    sum_b.values = tie(sum_b.values, output)
    sums.append(sum_b.cores_back())

    chips = groups // 2
    rows = model // (groups * parts)
    where = jnp.stack([own % 2, own // 2, place]).astype(i32)

    tail = extra_width + BLOCK
    widths = (3 * model, model, BLOCK, tail)

    def finish(team, a, b, olds):
        def piece_spec(width):
            return pl.BlockSpec((1, parts, rows, width), lambda s, at: (s, 0, 0, 0))

        def whole_spec(width):
            return pl.BlockSpec(
                (1, parts, rows, width),
                lambda s, at: ((at[0] ^ team) * chips + (at[1] ^ s), 0, 0, 0),
            )

        return pl.pallas_call(
            finish_kernel,
            grid_spec=pltpu.PrefetchScalarGridSpec(
                num_scalar_prefetch=1,
                grid=(chips,),
                in_specs=[
                    piece_spec(a.shape[-1]),
                    piece_spec(b.shape[-1]),
                    whole_spec(3 * model),
                ]
                + [any_space] * len(olds),
                out_specs=[whole_spec(width) for width in widths],
            ),
            out_shape=[shape((groups, parts, rows, width), f32) for width in widths],
            input_output_aliases={4 + n: n for n in range(len(olds))},
            compiler_params=params(("arbitrary",)),
            cost_estimate=cost(1e8, 1e7),
            name="finish",
        )(where, a, b, w_qkv.reshape(groups, parts, rows, 3 * model), *olds)

    (own_a, got_a), (own_b, got_b) = sums
    finished = finish(0, own_a, own_b, [])
    finished = finish(1, got_a, got_b, finished)
    grad_w_qkv, grad_w_out, gain_sums, extras = [
        item.reshape(model, item.shape[-1]) for item in finished
    ]
    grad_router, gains, grad_bias = pl.pallas_call(
        functools.partial(small_kernel, experts=experts, at=extra_width),
        out_shape=[
            shape((experts, model), f32),
            shape((2, model), f32),
            shape((head_count, bucket_count), f32),
        ],
        in_specs=[vmem] * 3,
        out_specs=[vmem] * 3,
        compiler_params=params(),
        cost_estimate=cost(1e6, 2e6),
        name="small",
    )(gain_one_row, gain_sums, extras)
    return (
        output,
        grad_tokens,
        gains[0],
        grad_w_qkv,
        grad_w_out,
        grad_bias.T,
        gains[1],
        grad_router.T,
        grad_w_in,
        grad_w_back,
    )


def solution(mesh):
    return jax.shard_map(
        local,
        mesh=mesh,
        in_specs=(
            P(("expert", "hidden"), None),
            P(("expert", "hidden"), None),
            P(("expert", "hidden"), None),
            P(("expert", "hidden")),
            P(("expert", "hidden")),
            P(("expert", "hidden")),
            P(),
            P(),
            P(),
            P(),
            P(),
            P(),
            P("expert", None, "hidden"),
            P("expert", "hidden", None),
        ),
        out_specs=(
            P(("expert", "hidden"), None),
            P(("expert", "hidden"), None),
            P(),
            P(),
            P(),
            P(),
            P(),
            P(),
            P("expert", None, "hidden"),
            P("expert", "hidden", None),
        ),
        check_vma=False,
    )
```

profile of v0, /device:TPU:9, one launch (start us, length us, event | category | flops | bytes accessed | tf_op | source)
XLA Modules:
  0.0 407.2 jit_solution(13545089777251097309)
XLA Ops:
  15.3 6.1 %qkv.1 = (bf16[512,2304]{1,0:T(8,128)(2,1)}, bf16[768,512]{1,0:T(8,128)(2,1)}) custom-call(bf16[512,768]{1,0:T(8,128)(2,1)} %refs_0_.1, f32[1,768]{1,0:T(1,128)} %broadcast_in_dim.15.gain_ref.refs_1_, bf16[768,2304]{1,0:T(8,128)(2,1)} %refs_2_.1), custom_call_target="tpu_custom_call" | custom-call | flops 18119392 | bytes 94371 | tf_op jit(solution)/shard_map/qkv/pallas_call | solution.py:700
  21.4 7.2 %attend.3 = (bf16[512,384]{1,0:T(8,128)(2,1)}, bf16[6,512,512]{2,1,0:T(8,128)(2,1)}) custom-call(bf16[512,2304]{1,0:T(8,128)(2,1)} %get-tuple-element.95.q_ref.k_ref.v_ref, bf16[512,2304]{1,0:T(8,128)(2,1)} %get-tuple-element.95.q_ref.k_ref.v_ref, bf16[512,2304]{1,0:T(8,128)(2,1)} %get-tuple-element.95.q_ref.k_ref.v_ref, ...), custom_call_target="tpu_custom_call" | custom-call | flops 120000000 | bytes 90000 | tf_op jit(solution)/shard_map/attend/pallas_call | solution.py:726
  28.6 7.2 %attend.2 = (bf16[512,384]{1,0:T(8,128)(2,1)}, bf16[6,512,512]{2,1,0:T(8,128)(2,1)}) custom-call(bf16[512,2304]{1,0:T(8,128)(2,1)} %get-tuple-element.95.q_ref.k_ref.v_ref, bf16[512,2304]{1,0:T(8,128)(2,1)} %get-tuple-element.95.q_ref.k_ref.v_ref, bf16[512,2304]{1,0:T(8,128)(2,1)} %get-tuple-element.95.q_ref.k_ref.v_ref, ...), custom_call_target="tpu_custom_call" | custom-call | flops 120000000 | bytes 90000 | tf_op jit(solution)/shard_map/attend/pallas_call | solution.py:726
  35.8 5.6 %route.1 = (f32[512,768]{1,0:T(8,128)}, f32[512,16]{1,0:T(8,128)}, bf16[8,2,40,768]{3,2,1,0:T(8,128)(2,1)}) custom-call(bf16[512,768]{1,0:T(8,128)(2,1)} %refs_0_.1, bf16[512,384]{1,0:T(8,128)(2,1)} %get-tuple-element.99.att_a_ref.refs_0_, bf16[512,384]{1,0:T(8,128)(2,1)} %get-tuple-element.100.att_b_ref.refs_1_, bf16[768,768]{1,0:T(8,128)(2,1)} %w_out_ref.3, ...), custom_call_target="tpu_custom_call" | custom-call | flops 60000000 | bytes 60000 | tf_op jit(solution)/shard_map/route/pallas_call | solution.py:758
  41.4 18.0 %all_to_all.36 = bf16[8,2,40,768]{3,2,1,0:T(8,128)(2,1)S(1)} all-to-all(bf16[8,2,40,768]{3,2,1,0:T(8,128)(2,1)} %get-tuple-element.103), channel_id=1, replica_groups=mesh['expert'=8,'hidden'=4] {'expert'}, dimensions={0} | all-to-all | bytes 1966080 | tf_op jit(solution)/shard_map/all_to_all | solution.py:684
  68.0 4.8 %all-gather.9.cloned.1.call-done = bf16[2048,768]{1,0:T(8,128)(2,1)} async-done(((bf16[512,768]{1,0:T(8,128)(2,1)}), bf16[2048,768]{1,0:T(8,128)(2,1)}) %all-gather.9.cloned.1.call-update) | async-done | bytes 3145744 | tf_op jit(solution)/shard_map/all_gather | solution.py:686
  82.5 4.7 %slots.3.refs_5_ = bf16[8,4,40,768]{3,2,1,0:T(8,128)(2,1)} custom-call(s32[1]{0:T(128)} %bitcast.6.refs_0_, s32[8,512]{1,0:T(8,128)} %get-tuple-element.104.row_ids_ref.rows_ref.refs_1_, s32[8,512]{1,0:T(8,128)} %copy-done.20, s32[8,512]{1,0:T(8,128)} %copy-done.21, s32[8,512]{1,0:T(8,128)} %copy-done.22, bf16[4,512,768]{2,1,0:T(8,128)(2,1)} %bitcast.112, ...), custom_call_target="tpu_custom_call" | custom-call | flops 20000000 | bytes 60000 | tf_op jit(solution)/shard_map/slots/pallas_call | solution.py:872
  87.2 16.4 %all-to-all-done.1 = bf16[8,4,40,768]{3,2,1,0:T(8,128)(2,1)S(1)} async-done(((bf16[8,4,40,768]{3,2,1,0:T(8,128)(2,1)}), bf16[8,4,40,768]{3,2,1,0:T(8,128)(2,1)S(1)}, u32[]{:S(2)}, u32[]{:S(2)}) %all-to-all-start.1) | async-done | bytes 1966112 | tf_op jit(solution)/shard_map/all_to_all | solution.py:684
  105.0 13.4 %all-gather.7.cloned.1.call-done.refs_1_ = bf16[4,320,768]{2,1,0:T(8,128)(2,1)} async-done(((bf16[1,320,768]{2,1,0:T(8,128)(2,1)}), bf16[4,320,768]{2,1,0:T(8,128)(2,1)}) %all-gather.7.cloned.1.call-update) | async-done | bytes 1966096 | tf_op jit(solution)/shard_map/all_gather | solution.py:889
  118.4 7.1 %experts.4 = (bf16[336,768]{1,0:T(8,128)(2,1)}, bf16[336,768]{1,0:T(8,128)(2,1)}, bf16[4,320,768]{2,1,0:T(8,128)(2,1)}, bf16[4,320,768]{2,1,0:T(8,128)(2,1)}) custom-call(s32[1]{0:T(128)} %bitcast.6.refs_0_, bf16[4,320,768]{2,1,0:T(8,128)(2,1)} %all-gather.7.cloned.1.call-done.refs_1_, bf16[4,320,768]{2,1,0:T(8,128)(2,1)} %bitcast.108, ...), custom_call_target="tpu_custom_call" | custom-call | flops 15099494 | bytes 100000 | tf_op jit(solution)/shard_map/experts/pallas_call | solution.py:782
  132.0 7.1 %experts.5 = (bf16[336,768]{1,0:T(8,128)(2,1)}, bf16[336,768]{1,0:T(8,128)(2,1)}, bf16[4,320,768]{2,1,0:T(8,128)(2,1)}, bf16[4,320,768]{2,1,0:T(8,128)(2,1)}) custom-call(s32[1]{0:T(128)} %bitcast.6.refs_0_, bf16[4,320,768]{2,1,0:T(8,128)(2,1)} %all-gather.7.cloned.1.call-done.refs_1_, ...), custom_call_target="tpu_custom_call", output_to_operand_aliasing={{2}: (5, {}), {3}: (6, {})} | custom-call | flops 15099494 | bytes 100000 | tf_op jit(solution)/shard_map/experts/pallas_call | solution.py:782
  139.1 11.1 %expert_weights.2 = (f32[2,768,768]{2,1,0:T(8,128)}, f32[2,768,768]{2,1,0:T(8,128)}, bf16[4,8,2,40,768]{4,3,2,1,0:T(8,128)(2,1)}) custom-call(s32[1]{0:T(128)} %bitcast.3.refs_0_, bf16[4,320,768]{2,1,0:T(8,128)(2,1)} %all-gather.7.cloned.1.call-done.refs_1_, bf16[4,320,768]{2,1,0:T(8,128)(2,1)} %bitcast.110, ...), custom_call_target="tpu_custom_call" | custom-call | flops 30198988 | bytes 130000 | tf_op jit(solution)/shard_map/expert_weights/pallas_call | solution.py:829
  153.0 5.2 %collective-permute-start.7 = (bf16[336,768]{1,0:T(8,128)(2,1)S(1)}, bf16[336,768]{1,0:T(8,128)(2,1)S(1)}, u32[]{:S(2)}, u32[]{:S(2)}) collective-permute-start(bf16[336,768]{1,0:T(8,128)(2,1)S(1)} %get-tuple-element.127), channel_id=1, source_target_pairs={{0,1},{1,2},{4,5},{5,6},{8,9},{9,10},{12,13},{13,14},{16,17},{17,1... | collective-permute-start | bytes 1548296 | tf_op jit(solution)/shard_map/ppermute | solution.py:577
  158.2 20.4 %collective-permute-done.8 = bf16[336,768]{1,0:T(8,128)(2,1)S(1)} collective-permute-done((bf16[336,768]{1,0:T(8,128)(2,1)S(1)}, bf16[336,768]{1,0:T(8,128)(2,1)S(1)}, u32[]{:S(2)}, u32[]{:S(2)}) %collective-permute-start.8) | collective-permute-done | bytes 516128 | tf_op jit(solution)/shard_map/ppermute | solution.py:579
  186.1 7.1 %experts.6 = (bf16[336,768]{1,0:T(8,128)(2,1)}, bf16[336,768]{1,0:T(8,128)(2,1)}, bf16[4,320,768]{2,1,0:T(8,128)(2,1)}, bf16[4,320,768]{2,1,0:T(8,128)(2,1)}) custom-call(s32[1]{0:T(128)} %bitcast.6.refs_0_, bf16[4,320,768]{2,1,0:T(8,128)(2,1)} %all-gather.5.cloned.1.call-done.refs_1_, bf16[4,320,768]{2,1,0:T(8,128)(2,1)} %bitcast.105, ...), custom_call_target="tpu_custom_call" | custom-call | flops 15099494 | bytes 100000 | tf_op jit(solution)/shard_map/experts/pallas_call | solution.py:782
  195.3 7.2 %experts.7 = (bf16[336,768]{1,0:T(8,128)(2,1)}, bf16[336,768]{1,0:T(8,128)(2,1)}, bf16[4,320,768]{2,1,0:T(8,128)(2,1)}, bf16[4,320,768]{2,1,0:T(8,128)(2,1)}) custom-call(s32[1]{0:T(128)} %bitcast.6.refs_0_, bf16[4,320,768]{2,1,0:T(8,128)(2,1)} %all-gather.5.cloned.1.call-done.refs_1_, ...), custom_call_target="tpu_custom_call", output_to_operand_aliasing={{2}: (5, {}), {3}: (6, {})} | custom-call | flops 15099494 | bytes 100000 | tf_op jit(solution)/shard_map/experts/pallas_call | solution.py:782
  209.3 5.1 %collective-permute-start.9 = (bf16[336,768]{1,0:T(8,128)(2,1)S(1)}, bf16[336,768]{1,0:T(8,128)(2,1)S(1)}, u32[]{:S(2)}, u32[]{:S(2)}) collective-permute-start(bf16[336,768]{1,0:T(8,128)(2,1)S(1)} %get-tuple-element.129), channel_id=1, source_target_pairs={{0,1},{1,2},{4,5},{5,6},{8,9},{9,10},{12,13},{13,14},{16,17},{17,1... | collective-permute-start | bytes 1548296 | tf_op jit(solution)/shard_map/ppermute | solution.py:577
  215.3 8.0 %all-to-all-start.4 = ((bf16[8,48,768]{2,1,0:T(8,128)(2,1)}), bf16[8,48,768]{2,1,0:T(8,128)(2,1)S(1)}, u32[]{:S(2)}, u32[]{:S(2)}) async-start(bf16[8,48,768]{2,1,0:T(8,128)(2,1)} %fusion.14), calls=%async_computation.5 | async-start | bytes 1179648 | tf_op jit(solution)/shard_map/all_to_all | solution.py:684
  230.0 11.1 %expert_weights.3 = (f32[2,768,768]{2,1,0:T(8,128)}, f32[2,768,768]{2,1,0:T(8,128)}, bf16[4,8,2,40,768]{4,3,2,1,0:T(8,128)(2,1)}) custom-call(s32[1]{0:T(128)} %bitcast.3.refs_0_, bf16[4,320,768]{2,1,0:T(8,128)(2,1)} %all-gather.5.cloned.1.call-done.refs_1_, ...), custom_call_target="tpu_custom_call", output_to_operand_aliasing={{0}: (7, {}), {1}: (8, {}), {2}: (9, {})} | custom-call | flops 30198988 | bytes 130000 | tf_op jit(solution)/shard_map/expert_weights/pallas_call | solution.py:829
  243.5 7.0 %all-to-all-start.5 = ((bf16[8,48,768]{2,1,0:T(8,128)(2,1)}), bf16[8,48,768]{2,1,0:T(8,128)(2,1)S(1)}, u32[]{:S(2)}, u32[]{:S(2)}) async-start(bf16[8,48,768]{2,1,0:T(8,128)(2,1)} %fusion.15), calls=%async_computation.6 | async-start | bytes 1179648 | tf_op jit(solution)/shard_map/all_to_all | solution.py:684
  250.5 7.0 %all-to-all-done.5 = bf16[8,48,768]{2,1,0:T(8,128)(2,1)S(1)} async-done(((bf16[8,48,768]{2,1,0:T(8,128)(2,1)}), bf16[8,48,768]{2,1,0:T(8,128)(2,1)S(1)}, u32[]{:S(2)}, u32[]{:S(2)}) %all-to-all-start.5) | async-done | bytes 589856 | tf_op jit(solution)/shard_map/all_to_all | solution.py:684
  258.4 9.0 %middle.1 = (f32[512,768]{1,0:T(8,128)}, bf16[512,768]{1,0:T(8,128)(2,1)}, bf16[512,768]{1,0:T(8,128)(2,1)}, bf16[768,128]{1,0:T(8,128)(2,1)}) custom-call(f32[512,768]{1,0:T(8,128)} %get-tuple-element.101.residual_ref, bf16[512,768]{1,0:T(8,128)(2,1)} %cot_ref.1, f32[1,768]{1,0:T(1,128)} %broadcast_in_dim.19.gain_ref, f32[768,16]{1,0:T(8,128)} %copy.47.w_router_ref.refs_4_, ...), custom_call_target="tpu_custom_call" | custom-call | flops 60000000 | bytes 80000 | tf_op jit(solution)/shard_map/middle/pallas_call | solution.py:926
  267.4 10.0 %attend_back.3 = (bf16[512,256]{1,0:T(8,128)(2,1)}, bf16[512,256]{1,0:T(8,128)(2,1)}, bf16[512,256]{1,0:T(8,128)(2,1)}, bf16[768,1664]{1,0:T(8,128)(2,1)}, f32[16,768]{1,0:T(8,128)}) custom-call(bf16[512,2304]{1,0:T(8,128)(2,1)} %get-tuple-element.95.q_ref.k_ref.v_ref, bf16[512,2304]{1,0:T(8,128)(2,1)} %get-tuple-element.95.q_ref.k_ref.v_ref, ...), custom_call_target="tpu_custom_call" | custom-call | flops 80000000 | bytes 60000 | tf_op jit(solution)/shard_map/attend_back/pallas_call | solution.py:956
  282.1 5.1 %attend_back.4 = (bf16[512,128]{1,0:T(8,128)(2,1)}, bf16[512,128]{1,0:T(8,128)(2,1)}, bf16[512,128]{1,0:T(8,128)(2,1)}, bf16[768,384]{1,0:T(8,128)(2,1)}, f32[16,768]{1,0:T(8,128)}) custom-call(bf16[512,2304]{1,0:T(8,128)(2,1)} %get-tuple-element.95.q_ref.k_ref.v_ref, bf16[512,2304]{1,0:T(8,128)(2,1)} %get-tuple-element.95.q_ref.k_ref.v_ref, ...), custom_call_target="tpu_custom_call" | custom-call | flops 40000000 | bytes 30000 | tf_op jit(solution)/shard_map/attend_back/pallas_call | solution.py:956
  290.4 12.2 %attend_back.5 = (bf16[512,384]{1,0:T(8,128)(2,1)}, bf16[512,384]{1,0:T(8,128)(2,1)}, bf16[512,384]{1,0:T(8,128)(2,1)}, bf16[768,1664]{1,0:T(8,128)(2,1)}, f32[16,768]{1,0:T(8,128)}) custom-call(bf16[512,2304]{1,0:T(8,128)(2,1)} %get-tuple-element.95.q_ref.k_ref.v_ref, bf16[512,2304]{1,0:T(8,128)(2,1)} %get-tuple-element.95.q_ref.k_ref.v_ref, ...), custom_call_target="tpu_custom_call" | custom-call | flops 120000000 | bytes 90000 | tf_op jit(solution)/shard_map/attend_back/pallas_call | solution.py:956
  319.6 6.4 %collective-permute-done.32 = bf16[96,1664]{1,0:T(8,128)(2,1)S(1)} collective-permute-done((bf16[96,1664]{1,0:T(8,128)(2,1)S(1)}, bf16[96,1664]{1,0:T(8,128)(2,1)S(1)}, u32[]{:S(2)}, u32[]{:S(2)}) %collective-permute-start.32) | collective-permute-done | bytes 319520 | tf_op jit(solution)/shard_map/ppermute | solution.py:624
  333.8 6.6 %all-to-all-start.3 = ((bf16[8,2,40,768]{3,2,1,0:T(8,128)(2,1)}), bf16[8,2,40,768]{3,2,1,0:T(8,128)(2,1)S(1)}, u32[]{:S(2)}, u32[]{:S(2)}) async-start(bf16[8,2,40,768]{3,2,1,0:T(8,128)(2,1)} %bitcast.143), calls=%async_computation.4 | async-start | bytes 1966080 | tf_op jit(solution)/shard_map/all_to_all | solution.py:684
  348.5 7.4 %tokens_grad.1 = f32[512,768]{1,0:T(8,128)} custom-call(bf16[512,768]{1,0:T(8,128)(2,1)} %refs_0_.1, f32[1,768]{1,0:T(1,128)} %broadcast_in_dim.15.gain_ref.refs_1_, bf16[768,2304]{1,0:T(8,128)(2,1)} %refs_2_.1, f32[512,768]{1,0:T(8,128)} %get-tuple-element.144.refs_3_, bf16[512,256]{1,0:T(8,128)(2,1)} %get-tuple-element.150.refs_4_, ...), custom_call_target="tpu_custom_call" | custom-call | flops 30000000 | bytes 100000 | tf_op jit(solution)/shard_map/tokens_grad/pallas_call | solution.py:1002
  361.4 6.6 %collective-permute-done.28 = bf16[4,24,1664]{2,1,0:T(8,128)(2,1)S(1)} collective-permute-done((bf16[4,24,1664]{2,1,0:T(8,128)(2,1)S(1)}, bf16[4,24,1664]{2,1,0:T(8,128)(2,1)S(1)}, u32[]{:S(2)}, u32[]{:S(2)}) %collective-permute-start.28) | collective-permute-done | bytes 319520 | tf_op jit(solution)/shard_map/ppermute | solution.py:648
  374.0 7.8 %collective-permute-done.41 = bf16[4,24,1664]{2,1,0:T(8,128)(2,1)S(1)} collective-permute-done((bf16[4,24,1664]{2,1,0:T(8,128)(2,1)S(1)}, bf16[4,24,1664]{2,1,0:T(8,128)(2,1)S(1)}, u32[]{:S(2)}, u32[]{:S(2)}) %collective-permute-start.41) | collective-permute-done | bytes 319520 | tf_op jit(solution)/shard_map/ppermute | solution.py:648
  383.5 5.8 %finish.2 = (f32[8,4,24,2304]{3,2,1,0:T(8,128)}, f32[8,4,24,768]{3,2,1,0:T(8,128)}, f32[8,4,24,128]{3,2,1,0:T(8,128)}, f32[8,4,24,256]{3,2,1,0:T(8,128)}) custom-call(s32[3]{0:T(128)} %pad_add_fusion.where_ref, bf16[4,4,24,1664]{3,2,1,0:T(8,128)(2,1)} %copy-done.1, bf16[4,4,24,1664]{3,2,1,0:T(8,128)(2,1)} %copy-done.2, bf16[8,4,24,2304]{3,2,1,0:T(8,128)(2,1)} %bitcast.103), custom_call_target="tpu_custom_call" | custom-call | flops 1000000 | bytes 100000 | tf_op jit(solution)/shard_map/finish/pallas_call | solution.py:1040
  390.8 5.8 %finish.3 = (f32[8,4,24,2304]{3,2,1,0:T(8,128)}, f32[8,4,24,768]{3,2,1,0:T(8,128)}, f32[8,4,24,128]{3,2,1,0:T(8,128)}, f32[8,4,24,256]{3,2,1,0:T(8,128)}) custom-call(s32[3]{0:T(128)} %pad_add_fusion.where_ref, bf16[4,4,24,1664]{3,2,1,0:T(8,128)(2,1)} %copy-done.8, ...), custom_call_target="tpu_custom_call", output_to_operand_aliasing={{0}: (4, {}), {1}: (5, {}), {2}: (6, {}), {3}: (7, {})} | custom-call | flops 1000000 | bytes 100000 | tf_op jit(solution)/shard_map/finish/pallas_call | solution.py:1040
  (188 shorter events, 122.8 us)
Async XLA Ops:
  7.2 65.7 %all-gather.9.cloned.1.call-start = ((), (), s32[]{:S(2)}) async-start(), calls=%async_computation.10 | async-start | bytes 3932160 | tf_op jit(solution)/shard_map/all_gather | solution.py:686
  7.9 110.5 %all-gather.7.cloned.1.call-start = ((), (), s32[]{:S(2)}) async-start(), calls=%async_computation.8 | async-start | bytes 2457600 | tf_op jit(solution)/shard_map/all_gather | solution.py:889
  77.3 26.3 %all-to-all-start.1 = ((bf16[8,4,40,768]{3,2,1,0:T(8,128)(2,1)}), bf16[8,4,40,768]{3,2,1,0:T(8,128)(2,1)S(1)}, u32[]{:S(2)}, u32[]{:S(2)}) async-start(bf16[8,4,40,768]{3,2,1,0:T(8,128)(2,1)} %slots.2.refs_6_), calls=%async_computation.1 | async-start | bytes 3932160 | tf_op jit(solution)/shard_map/all_to_all | solution.py:684
  81.8 104.4 %all-gather.5.cloned.1.call-start = ((), (), s32[]{:S(2)}) async-start(), calls=%async_computation.7 | async-start | bytes 2457600 | tf_op jit(solution)/shard_map/all_gather | solution.py:889
  125.5 26.0 %collective-permute-start.5 = (bf16[336,768]{1,0:T(8,128)(2,1)}, bf16[336,768]{1,0:T(8,128)(2,1)S(1)}, u32[]{:S(2)}, u32[]{:S(2)}) collective-permute-start(bf16[336,768]{1,0:T(8,128)(2,1)} %get-tuple-element.125), channel_id=1, source_target_pairs={{0,1},{4,5},{8,9},{12,13},{16,17},{20,21},{24,25},{28,29}} | collective-permute-start | bytes 1548296 | tf_op jit(solution)/shard_map/ppermute | solution.py:577
  126.8 24.7 %collective-permute-start.6 = (bf16[336,768]{1,0:T(8,128)(2,1)}, bf16[336,768]{1,0:T(8,128)(2,1)S(1)}, u32[]{:S(2)}, u32[]{:S(2)}) collective-permute-start(bf16[336,768]{1,0:T(8,128)(2,1)} %get-tuple-element.126), channel_id=1, source_target_pairs={{3,2},{7,6},{11,10},{15,14},{19,18},{23,22},{27,26},{31,30}} | collective-permute-start | bytes 1548296 | tf_op jit(solution)/shard_map/ppermute | solution.py:579
  127.5 57.3 %all-to-all-start.2 = ((bf16[8,4,40,768]{3,2,1,0:T(8,128)(2,1)}), bf16[8,4,40,768]{3,2,1,0:T(8,128)(2,1)S(1)}, u32[]{:S(2)}, u32[]{:S(2)}) async-start(bf16[8,4,40,768]{3,2,1,0:T(8,128)(2,1)} %slots.3.refs_5_), calls=%async_computation.2 | async-start | bytes 3932160 | tf_op jit(solution)/shard_map/all_to_all | solution.py:684
  151.7 26.9 %collective-permute-start.8 = (bf16[336,768]{1,0:T(8,128)(2,1)S(1)}, bf16[336,768]{1,0:T(8,128)(2,1)S(1)}, u32[]{:S(2)}, u32[]{:S(2)}) collective-permute-start(bf16[336,768]{1,0:T(8,128)(2,1)S(1)} %get-tuple-element.128), channel_id=1, source_target_pairs={{2,1},{3,2},{6,5},{7,6},{10,9},{11,10},{14,13},{15,14},{18,17},{19... | collective-permute-start | bytes 1548296 | tf_op jit(solution)/shard_map/ppermute | solution.py:579
  153.0 25.9 %collective-permute-start.7 = (bf16[336,768]{1,0:T(8,128)(2,1)S(1)}, bf16[336,768]{1,0:T(8,128)(2,1)S(1)}, u32[]{:S(2)}, u32[]{:S(2)}) collective-permute-start(bf16[336,768]{1,0:T(8,128)(2,1)S(1)} %get-tuple-element.127), channel_id=1, source_target_pairs={{0,1},{1,2},{4,5},{5,6},{8,9},{9,10},{12,13},{13,14},{16,17},{17,1... | collective-permute-start | bytes 1548296 | tf_op jit(solution)/shard_map/ppermute | solution.py:577
  179.0 16.2 %collective-permute-start.10 = (bf16[336,768]{1,0:T(8,128)(2,1)S(1)}, bf16[336,768]{1,0:T(8,128)(2,1)S(1)}, u32[]{:S(2)}, u32[]{:S(2)}) collective-permute-start(bf16[336,768]{1,0:T(8,128)(2,1)S(1)} %add_convert_fusion.5), channel_id=1, source_target_pairs={{0,1},{1,2},{2,3},{4,5},{5,6},{6,7},{8,9},{9,10},{10,11},{12,13},{... | collective-permute-start | bytes 1548296 | tf_op jit(solution)/shard_map/ppermute | solution.py:577
  206.7 16.6 %collective-permute-start.12 = (bf16[336,768]{1,0:T(8,128)(2,1)S(1)}, bf16[336,768]{1,0:T(8,128)(2,1)}, u32[]{:S(2)}, u32[]{:S(2)}) collective-permute-start(bf16[336,768]{1,0:T(8,128)(2,1)S(1)} %get-tuple-element.137), channel_id=1, source_target_pairs={{2,1},{3,2},{6,5},{7,6},{10,9},{11,10},{14,13},{15,14},{18,17},{19... | collective-permute-start | bytes 1548296 | tf_op jit(solution)/shard_map/ppermute | solution.py:579
  209.3 15.2 %collective-permute-start.9 = (bf16[336,768]{1,0:T(8,128)(2,1)S(1)}, bf16[336,768]{1,0:T(8,128)(2,1)S(1)}, u32[]{:S(2)}, u32[]{:S(2)}) collective-permute-start(bf16[336,768]{1,0:T(8,128)(2,1)S(1)} %get-tuple-element.129), channel_id=1, source_target_pairs={{0,1},{1,2},{4,5},{5,6},{8,9},{9,10},{12,13},{13,14},{16,17},{17,1... | collective-permute-start | bytes 1548296 | tf_op jit(solution)/shard_map/ppermute | solution.py:577
  215.3 25.8 %all-to-all-start.4 = ((bf16[8,48,768]{2,1,0:T(8,128)(2,1)}), bf16[8,48,768]{2,1,0:T(8,128)(2,1)S(1)}, u32[]{:S(2)}, u32[]{:S(2)}) async-start(bf16[8,48,768]{2,1,0:T(8,128)(2,1)} %fusion.14), calls=%async_computation.5 | async-start | bytes 1179648 | tf_op jit(solution)/shard_map/all_to_all | solution.py:684
  223.3 110.5 %reduce-scatter.2.cloned.1.call-start = ((), (), s32[]{:S(2)}) async-start(), calls=%async_computation.9 | async-start | bytes 4915200 | tf_op jit(solution)/shard_map/reduce_scatter | solution.py:941
  224.7 16.5 %collective-permute-start.13 = (bf16[336,768]{1,0:T(8,128)(2,1)S(1)}, bf16[336,768]{1,0:T(8,128)(2,1)S(1)}, u32[]{:S(2)}, u32[]{:S(2)}) collective-permute-start(bf16[336,768]{1,0:T(8,128)(2,1)S(1)} %add_convert_fusion.2), channel_id=1, source_target_pairs={{0,1},{1,2},{2,3},{4,5},{5,6},{6,7},{8,9},{9,10},{10,11},{12,13},{... | collective-permute-start | bytes 1548296 | tf_op jit(solution)/shard_map/ppermute | solution.py:577
  226.6 14.6 %collective-permute-start.14 = (bf16[336,768]{1,0:T(8,128)(2,1)S(1)}, bf16[336,768]{1,0:T(8,128)(2,1)S(1)}, u32[]{:S(2)}, u32[]{:S(2)}) collective-permute-start(bf16[336,768]{1,0:T(8,128)(2,1)S(1)} %add_convert_fusion.1), channel_id=1, source_target_pairs={{1,0},{2,1},{3,2},{5,4},{6,5},{7,6},{9,8},{10,9},{11,10},{13,12},{... | collective-permute-start | bytes 1548296 | tf_op jit(solution)/shard_map/ppermute | solution.py:579
  243.5 14.0 %all-to-all-start.5 = ((bf16[8,48,768]{2,1,0:T(8,128)(2,1)}), bf16[8,48,768]{2,1,0:T(8,128)(2,1)S(1)}, u32[]{:S(2)}, u32[]{:S(2)}) async-start(bf16[8,48,768]{2,1,0:T(8,128)(2,1)} %fusion.15), calls=%async_computation.6 | async-start | bytes 1179648 | tf_op jit(solution)/shard_map/all_to_all | solution.py:684
  287.6 14.9 %collective-permute-start.16 = (bf16[96,1664]{1,0:T(8,128)(2,1)S(1)}, bf16[96,1664]{1,0:T(8,128)(2,1)S(1)}, u32[]{:S(2)}, u32[]{:S(2)}) collective-permute-start(bf16[96,1664]{1,0:T(8,128)(2,1)S(1)} %get-tuple-element.185), channel_id=1, source_target_pairs={{0,8},{4,12},{8,0},{12,4},{16,24},{20,28},{24,16},{28,20},{1,9},{5... | collective-permute-start | bytes 958472 | tf_op jit(solution)/shard_map/ppermute | solution.py:624
  288.0 14.5 %collective-permute-start.17 = (bf16[96,1664]{1,0:T(8,128)(2,1)S(1)}, bf16[96,1664]{1,0:T(8,128)(2,1)S(1)}, u32[]{:S(2)}, u32[]{:S(2)}) collective-permute-start(bf16[96,1664]{1,0:T(8,128)(2,1)S(1)} %get-tuple-element.187), channel_id=1, source_target_pairs={{0,16},{4,20},{8,24},{12,28},{16,0},{20,4},{24,8},{28,12},{1,17},{... | collective-permute-start | bytes 958472 | tf_op jit(solution)/shard_map/ppermute | solution.py:624
  288.4 15.3 %collective-permute-start.18 = (bf16[96,1664]{1,0:T(8,128)(2,1)S(1)}, bf16[96,1664]{1,0:T(8,128)(2,1)S(1)}, u32[]{:S(2)}, u32[]{:S(2)}) collective-permute-start(bf16[96,1664]{1,0:T(8,128)(2,1)S(1)} %get-tuple-element.186), channel_id=1, source_target_pairs={{0,24},{4,28},{8,16},{12,20},{16,8},{20,12},{24,0},{28,4},{1,25},{... | collective-permute-start | bytes 958472 | tf_op jit(solution)/shard_map/ppermute | solution.py:624
  311.3 14.7 %collective-permute-start.32 = (bf16[96,1664]{1,0:T(8,128)(2,1)S(1)}, bf16[96,1664]{1,0:T(8,128)(2,1)S(1)}, u32[]{:S(2)}, u32[]{:S(2)}) collective-permute-start(bf16[96,1664]{1,0:T(8,128)(2,1)S(1)} %get-tuple-element.183), channel_id=1, source_target_pairs={{0,24},{4,28},{8,16},{12,20},{16,8},{20,12},{24,0},{28,4},{1,25},{... | collective-permute-start | bytes 958472 | tf_op jit(solution)/shard_map/ppermute | solution.py:624
  312.5 15.6 %collective-permute-start.20 = (bf16[24,1664]{1,0:T(8,128)(2,1)S(1)}, bf16[24,1664]{1,0:T(8,128)(2,1)S(1)}, u32[]{:S(2)}, u32[]{:S(2)}) collective-permute-start(bf16[24,1664]{1,0:T(8,128)(2,1)S(1)} %get-tuple-element.199), channel_id=1, source_target_pairs={{0,1},{1,2},{2,3},{3,0},{4,5},{5,6},{6,7},{7,4},{8,9},{9,10},{10,1... | collective-permute-start | bytes 239624 | tf_op jit(solution)/shard_map/ppermute | solution.py:633
  314.3 15.0 %collective-permute-start.21 = (bf16[24,1664]{1,0:T(8,128)(2,1)S(1)}, bf16[24,1664]{1,0:T(8,128)(2,1)S(1)}, u32[]{:S(2)}, u32[]{:S(2)}) collective-permute-start(bf16[24,1664]{1,0:T(8,128)(2,1)S(1)} %get-tuple-element.201), channel_id=1, source_target_pairs={{0,2},{1,3},{2,0},{3,1},{4,6},{5,7},{6,4},{7,5},{8,10},{9,11},{10,... | collective-permute-start | bytes 239624 | tf_op jit(solution)/shard_map/ppermute | solution.py:633
  326.2 14.1 %collective-permute-start.33 = (bf16[24,1664]{1,0:T(8,128)(2,1)S(1)}, bf16[24,1664]{1,0:T(8,128)(2,1)S(1)}, u32[]{:S(2)}, u32[]{:S(2)}) collective-permute-start(bf16[24,1664]{1,0:T(8,128)(2,1)S(1)} %get-tuple-element.194), channel_id=1, source_target_pairs={{0,1},{1,2},{2,3},{3,0},{4,5},{5,6},{6,7},{7,4},{8,9},{9,10},{10,1... | collective-permute-start | bytes 239624 | tf_op jit(solution)/shard_map/ppermute | solution.py:633
  333.8 22.2 %all-to-all-start.3 = ((bf16[8,2,40,768]{3,2,1,0:T(8,128)(2,1)}), bf16[8,2,40,768]{3,2,1,0:T(8,128)(2,1)S(1)}, u32[]{:S(2)}, u32[]{:S(2)}) async-start(bf16[8,2,40,768]{3,2,1,0:T(8,128)(2,1)} %bitcast.143), calls=%async_computation.4 | async-start | bytes 1966080 | tf_op jit(solution)/shard_map/all_to_all | solution.py:684
  344.3 15.9 %collective-permute-start.26 = (bf16[4,24,1664]{2,1,0:T(8,128)(2,1)S(1)}, bf16[4,24,1664]{2,1,0:T(8,128)(2,1)S(1)}, u32[]{:S(2)}, u32[]{:S(2)}) collective-permute-start(bf16[4,24,1664]{2,1,0:T(8,128)(2,1)S(1)} %get-tuple-element.198), channel_id=1, source_target_pairs={{0,8},{4,12},{8,0},{12,4},{16,24},{20,28},{24,16},{28,20},{1,9},{5... | collective-permute-start | bytes 958472 | tf_op jit(solution)/shard_map/ppermute | solution.py:648
  347.1 14.4 %collective-permute-start.27 = (bf16[4,24,1664]{2,1,0:T(8,128)(2,1)S(1)}, bf16[4,24,1664]{2,1,0:T(8,128)(2,1)S(1)}, u32[]{:S(2)}, u32[]{:S(2)}) collective-permute-start(bf16[4,24,1664]{2,1,0:T(8,128)(2,1)S(1)} %get-tuple-element.198), channel_id=1, source_target_pairs={{0,16},{4,20},{8,24},{12,28},{16,0},{20,4},{24,8},{28,12},{1,17},{... | collective-permute-start | bytes 958472 | tf_op jit(solution)/shard_map/ppermute | solution.py:648
  348.3 19.8 %collective-permute-start.28 = (bf16[4,24,1664]{2,1,0:T(8,128)(2,1)S(1)}, bf16[4,24,1664]{2,1,0:T(8,128)(2,1)S(1)}, u32[]{:S(2)}, u32[]{:S(2)}) collective-permute-start(bf16[4,24,1664]{2,1,0:T(8,128)(2,1)S(1)} %get-tuple-element.198), channel_id=1, source_target_pairs={{0,24},{4,28},{8,16},{12,20},{16,8},{20,12},{24,0},{28,4},{1,25},{... | collective-permute-start | bytes 958472 | tf_op jit(solution)/shard_map/ppermute | solution.py:648
  357.0 17.0 %collective-permute-start.39 = (bf16[4,24,1664]{2,1,0:T(8,128)(2,1)S(1)}, bf16[4,24,1664]{2,1,0:T(8,128)(2,1)S(1)}, u32[]{:S(2)}, u32[]{:S(2)}) collective-permute-start(bf16[4,24,1664]{2,1,0:T(8,128)(2,1)S(1)} %pad_maximum_fusion.3), channel_id=1, source_target_pairs={{0,8},{4,12},{8,0},{12,4},{16,24},{20,28},{24,16},{28,20},{1,9},{5... | collective-permute-start | bytes 958472 | tf_op jit(solution)/shard_map/ppermute | solution.py:648
  358.2 15.8 %collective-permute-start.40 = (bf16[4,24,1664]{2,1,0:T(8,128)(2,1)S(1)}, bf16[4,24,1664]{2,1,0:T(8,128)(2,1)S(1)}, u32[]{:S(2)}, u32[]{:S(2)}) collective-permute-start(bf16[4,24,1664]{2,1,0:T(8,128)(2,1)S(1)} %pad_maximum_fusion.3), channel_id=1, source_target_pairs={{0,16},{4,20},{8,24},{12,28},{16,0},{20,4},{24,8},{28,12},{1,17},{... | collective-permute-start | bytes 958472 | tf_op jit(solution)/shard_map/ppermute | solution.py:648
  360.2 21.5 %collective-permute-start.41 = (bf16[4,24,1664]{2,1,0:T(8,128)(2,1)S(1)}, bf16[4,24,1664]{2,1,0:T(8,128)(2,1)S(1)}, u32[]{:S(2)}, u32[]{:S(2)}) collective-permute-start(bf16[4,24,1664]{2,1,0:T(8,128)(2,1)S(1)} %pad_maximum_fusion.3), channel_id=1, source_target_pairs={{0,24},{4,28},{8,16},{12,20},{16,8},{20,12},{24,0},{28,4},{1,25},{... | collective-permute-start | bytes 958472 | tf_op jit(solution)/shard_map/ppermute | solution.py:648
  368.2 21.1 %collective-permute-start.29 = (bf16[4,4,24,1664]{3,2,1,0:T(8,128)(2,1)S(1)}, bf16[4,4,24,1664]{3,2,1,0:T(8,128)(2,1)S(1)}, u32[]{:S(2)}, u32[]{:S(2)}) collective-permute-start(bf16[4,4,24,1664]{3,2,1,0:T(8,128)(2,1)S(1)} %pad_maximum_fusion.a_ref), channel_id=1, source_target_pairs={{0,4},{4,0},{8,12},{12,8},{16,20},{20,16},{24,28},{28,24},{1,5},{5... | collective-permute-start | bytes 3833864 | tf_op jit(solution)/shard_map/ppermute | solution.py:652
  (43 other events, 349.1 us)
Sparse Core Ops, SparseCore 0:
  9.6 63.2 all-gather.8
  75.0 43.3 all-gather.6
  120.0 64.5 all-gather.4
  241.2 75.6 reduce-scatter.1
where the time goes:
time: 415 us; the launch traced here: 407 us
  Pallas kernels  149 us (36%)
  waiting for transfers between devices  103 us (25%)
  starting transfers between devices  94.6 us (23%)
  local copies, waits for them, and re-layouts  19.8 us (5%)
  blocking collectives  18 us (4%)
  between operations  14.8 us (4%)
  other arithmetic  8.48 us (2%)
    all_to_all x5, starting transfers between devices, exchange(): lax.all_to_all(rows, 'expert', split_axis=axis, concat_axis=axis, tiled=T...  30.6 us
    pallas_call x4, Pallas kernels, run_experts(): pl.pallas_call(held(functools.partial(expert_kernel, parts=parts, le=le,...  28.5 us
    pallas_call x3, Pallas kernels, run_back(): pl.pallas_call(functools.partial(attend_back_kernel, kind=kind, head_star...  27.3 us
    all_to_all x5, waiting for transfers between devices, exchange(): lax.all_to_all(rows, 'expert', split_axis=axis, concat_axis=axis, tiled=T...  23.5 us
    pallas_call x2, Pallas kernels, run_weights(): pl.pallas_call(held(functools.partial(expert_weights_kernel, le=le, local...  22.2 us
    ppermute x6, waiting for transfers between devices, step(): self.left = lax.ppermute(left, 'hidden', ways)  20.4 us
    ppermute x6, starting transfers between devices, step(): self.right = lax.ppermute(right, 'hidden', ways)  18.4 us
    all_to_all x1, blocking collectives, exchange(): lax.all_to_all(rows, 'expert', split_axis=axis, concat_axis=axis, tiled=T...  18 us
  transfers between devices with their start and end apart: 52, of which 20 were waited for; matrix products, arithmetic and copies ran while one was open for 5% of the time, Pallas kernels for 35%

commit v1 on v0

--- a/solution.py
+++ b/solution.py
@@ -314,8 +314,8 @@
 
 
 def middle_kernel(residual_ref, cot_ref, gain_ref, w_router_ref, router_ref, cols_ref, w_out_ref, *refs, capacity, stride):
-    grad_res_ref, branch_ref, att_ref, extra_ref = refs[-4:]
-    back_refs = refs[:-4]
+    grad_res_ref, branch_ref, att_ref, extra_ref, sums_ref = refs[-5:]
+    back_refs = refs[:-5]
     local_experts = len(back_refs)
     tokens = residual_ref.shape[0]
     rows = None
@@ -359,11 +359,23 @@
     experts = logits_high.shape[1]
     router_grad = mm(jnp.concatenate([logits_high, logits_low], axis=1), normed_high, TN)
     router_grad = router_grad[:experts] + router_grad[experts:] + mm(logits_high, normed_low, TN)
-    spare = extra_ref.shape[1] - router_grad.shape[0] - 1
+    spare = sums_ref.shape[0] - router_grad.shape[0] - 1
     both = jnp.concatenate(
         [router_grad, gain_grad, jnp.zeros((spare, gain_grad.shape[1]), f32)], axis=0
     )
-    extra_ref[...] = both.T.astype(bf16)
+    step = pl.program_id(0)
+
+    @pl.when(step == 0)
+    def _():
+        sums_ref[...] = both
+
+    @pl.when(step > 0)
+    def _():
+        sums_ref[...] += both
+
+    @pl.when(step == pl.num_programs(0) - 1)
+    def _():
+        extra_ref[...] = sums_ref[...].T.astype(bf16)
 
 
 def attend_back_kernel(q_ref, k_ref, v_ref, probs_ref, grad_ref, turned_ref, *refs, kind, head_start, buckets):
@@ -923,20 +935,51 @@
     grad_w_in, grad_w_back, out_sums = grads
     extra_width = -(-(experts + 1) // BLOCK) * BLOCK
 
+    def token_spec(width):
+        return pl.BlockSpec((tok_rows // 2, width), lambda t: (t, 0))
+
+    def full_spec(item):
+        return pl.BlockSpec(item.shape, lambda t: (0, 0))
+
     grad_res, grad_branch, grad_att, extra = pl.pallas_call(
         functools.partial(middle_kernel, capacity=capacity, stride=stride),
+        grid=(2,),
         out_shape=[
             shape((tok_rows, model), f32),
             shape((tok_rows, model), bf16),
             shape((tok_rows, model), bf16),
             shape((model, extra_width), bf16),
         ],
-        in_specs=[vmem] * (7 + local_experts),
-        out_specs=[vmem] * 4,
-        compiler_params=params(),
+        in_specs=[
+            token_spec(model),
+            token_spec(model),
+            full_spec(gain_two_row),
+            full_spec(w_router),
+            token_spec(experts),
+            token_spec(BLOCK),
+            full_spec(w_out),
+            *[full_spec(item) for item in backs],
+        ],
+        out_specs=[
+            token_spec(model),
+            token_spec(model),
+            token_spec(model),
+            pl.BlockSpec((model, extra_width), lambda t: (0, 0)),
+        ],
+        scratch_shapes=[pltpu.VMEM((extra_width, model), f32)],
+        compiler_params=params(("arbitrary",)),
         cost_estimate=cost(6e9, 8e6),
         name="middle",
-    )(residual, cotangent, gain_two_row, w_router, router, id_cols, w_out, *backs)
+    )(
+        residual,
+        cotangent,
+        gain_two_row,
+        w_router,
+        router,
+        id_cols,
+        w_out,
+        *backs,
+    )
 
     out_rows = lax.psum_scatter(out_sums, "hidden", scatter_dimension=0, tiled=False)
     out_ready = out_rows

time: 415 us -> 415 us (level)
  no operation moved by 1% of the time
where the time goes in v1:
time: 415 us; the launch traced here: 407 us
  Pallas kernels  149 us (36%)
  waiting for transfers between devices  103 us (25%)
  starting transfers between devices  94.6 us (23%)
  local copies, waits for them, and re-layouts  19.8 us (5%)
  blocking collectives  18 us (4%)
  between operations  14.8 us (4%)
  other arithmetic  8.48 us (2%)
    all_to_all x5, starting transfers between devices, exchange(): lax.all_to_all(rows, 'expert', split_axis=axis, concat_axis=axis, tiled=T...  30.6 us
    pallas_call x4, Pallas kernels, run_experts(): pl.pallas_call(held(functools.partial(expert_kernel, parts=parts, le=le,...  28.5 us
    pallas_call x3, Pallas kernels, run_back(): pl.pallas_call(functools.partial(attend_back_kernel, kind=kind, head_star...  27.3 us
    all_to_all x5, waiting for transfers between devices, exchange(): lax.all_to_all(rows, 'expert', split_axis=axis, concat_axis=axis, tiled=T...  23.5 us
    pallas_call x2, Pallas kernels, run_weights(): pl.pallas_call(held(functools.partial(expert_weights_kernel, le=le, local...  22.2 us
    ppermute x6, waiting for transfers between devices, step(): self.left = lax.ppermute(left, 'hidden', ways)  20.4 us
    ppermute x6, starting transfers between devices, step(): self.right = lax.ppermute(right, 'hidden', ways)  18.4 us
    all_to_all x1, blocking collectives, exchange(): lax.all_to_all(rows, 'expert', split_axis=axis, concat_axis=axis, tiled=T...  18 us
  transfers between devices with their start and end apart: 52, of which 20 were waited for; matrix products, arithmetic and copies ran while one was open for 5% of the time, Pallas kernels for 35%

profile of v1, /device:TPU:9, one launch (start us, length us, event | category | flops | bytes accessed | tf_op | source)
XLA Modules:
  0.0 407.0 jit_solution(8921962575433789191)
XLA Ops:
  15.3 6.1 %qkv.1 = (bf16[512,2304]{1,0:T(8,128)(2,1)}, bf16[768,512]{1,0:T(8,128)(2,1)}) custom-call(bf16[512,768]{1,0:T(8,128)(2,1)} %refs_0_.1, f32[1,768]{1,0:T(1,128)} %broadcast_in_dim.15.gain_ref.refs_1_, bf16[768,2304]{1,0:T(8,128)(2,1)} %refs_2_.1), custom_call_target="tpu_custom_call" | custom-call | flops 18119392 | bytes 94371 | tf_op jit(solution)/shard_map/qkv/pallas_call | solution.py:712
  21.4 7.2 %attend.3 = (bf16[512,384]{1,0:T(8,128)(2,1)}, bf16[6,512,512]{2,1,0:T(8,128)(2,1)}) custom-call(bf16[512,2304]{1,0:T(8,128)(2,1)} %get-tuple-element.95.q_ref.k_ref.v_ref, bf16[512,2304]{1,0:T(8,128)(2,1)} %get-tuple-element.95.q_ref.k_ref.v_ref, bf16[512,2304]{1,0:T(8,128)(2,1)} %get-tuple-element.95.q_ref.k_ref.v_ref, ...), custom_call_target="tpu_custom_call" | custom-call | flops 120000000 | bytes 90000 | tf_op jit(solution)/shard_map/attend/pallas_call | solution.py:738
  28.6 7.2 %attend.2 = (bf16[512,384]{1,0:T(8,128)(2,1)}, bf16[6,512,512]{2,1,0:T(8,128)(2,1)}) custom-call(bf16[512,2304]{1,0:T(8,128)(2,1)} %get-tuple-element.95.q_ref.k_ref.v_ref, bf16[512,2304]{1,0:T(8,128)(2,1)} %get-tuple-element.95.q_ref.k_ref.v_ref, bf16[512,2304]{1,0:T(8,128)(2,1)} %get-tuple-element.95.q_ref.k_ref.v_ref, ...), custom_call_target="tpu_custom_call" | custom-call | flops 120000000 | bytes 90000 | tf_op jit(solution)/shard_map/attend/pallas_call | solution.py:738
  35.8 5.6 %route.1 = (f32[512,768]{1,0:T(8,128)}, f32[512,16]{1,0:T(8,128)}, bf16[8,2,40,768]{3,2,1,0:T(8,128)(2,1)}) custom-call(bf16[512,768]{1,0:T(8,128)(2,1)} %refs_0_.1, bf16[512,384]{1,0:T(8,128)(2,1)} %get-tuple-element.99.att_a_ref.refs_0_, bf16[512,384]{1,0:T(8,128)(2,1)} %get-tuple-element.100.att_b_ref.refs_1_, bf16[768,768]{1,0:T(8,128)(2,1)} %w_out_ref.3, ...), custom_call_target="tpu_custom_call" | custom-call | flops 60000000 | bytes 60000 | tf_op jit(solution)/shard_map/route/pallas_call | solution.py:770
  41.4 18.0 %all_to_all.36 = bf16[8,2,40,768]{3,2,1,0:T(8,128)(2,1)S(1)} all-to-all(bf16[8,2,40,768]{3,2,1,0:T(8,128)(2,1)} %get-tuple-element.103), channel_id=1, replica_groups=mesh['expert'=8,'hidden'=4] {'expert'}, dimensions={0} | all-to-all | bytes 1966080 | tf_op jit(solution)/shard_map/all_to_all | solution.py:696
  68.0 4.8 %all-gather.9.cloned.1.call-done = bf16[2048,768]{1,0:T(8,128)(2,1)} async-done(((bf16[512,768]{1,0:T(8,128)(2,1)}), bf16[2048,768]{1,0:T(8,128)(2,1)}) %all-gather.9.cloned.1.call-update) | async-done | bytes 3145744 | tf_op jit(solution)/shard_map/all_gather | solution.py:698
  82.5 4.7 %slots.3.refs_5_ = bf16[8,4,40,768]{3,2,1,0:T(8,128)(2,1)} custom-call(s32[1]{0:T(128)} %bitcast.6.refs_0_, s32[8,512]{1,0:T(8,128)} %get-tuple-element.104.row_ids_ref.rows_ref.refs_1_, s32[8,512]{1,0:T(8,128)} %copy-done.20, s32[8,512]{1,0:T(8,128)} %copy-done.21, s32[8,512]{1,0:T(8,128)} %copy-done.22, bf16[4,512,768]{2,1,0:T(8,128)(2,1)} %bitcast.112, ...), custom_call_target="tpu_custom_call" | custom-call | flops 20000000 | bytes 60000 | tf_op jit(solution)/shard_map/slots/pallas_call | solution.py:884
  87.2 16.4 %all-to-all-done.1 = bf16[8,4,40,768]{3,2,1,0:T(8,128)(2,1)S(1)} async-done(((bf16[8,4,40,768]{3,2,1,0:T(8,128)(2,1)}), bf16[8,4,40,768]{3,2,1,0:T(8,128)(2,1)S(1)}, u32[]{:S(2)}, u32[]{:S(2)}) %all-to-all-start.1) | async-done | bytes 1966112 | tf_op jit(solution)/shard_map/all_to_all | solution.py:696
  105.0 13.4 %all-gather.7.cloned.1.call-done.refs_1_ = bf16[4,320,768]{2,1,0:T(8,128)(2,1)} async-done(((bf16[1,320,768]{2,1,0:T(8,128)(2,1)}), bf16[4,320,768]{2,1,0:T(8,128)(2,1)}) %all-gather.7.cloned.1.call-update) | async-done | bytes 1966096 | tf_op jit(solution)/shard_map/all_gather | solution.py:901
  118.4 7.1 %experts.4 = (bf16[336,768]{1,0:T(8,128)(2,1)}, bf16[336,768]{1,0:T(8,128)(2,1)}, bf16[4,320,768]{2,1,0:T(8,128)(2,1)}, bf16[4,320,768]{2,1,0:T(8,128)(2,1)}) custom-call(s32[1]{0:T(128)} %bitcast.6.refs_0_, bf16[4,320,768]{2,1,0:T(8,128)(2,1)} %all-gather.7.cloned.1.call-done.refs_1_, bf16[4,320,768]{2,1,0:T(8,128)(2,1)} %bitcast.108, ...), custom_call_target="tpu_custom_call" | custom-call | flops 15099494 | bytes 100000 | tf_op jit(solution)/shard_map/experts/pallas_call | solution.py:794
  132.0 7.1 %experts.5 = (bf16[336,768]{1,0:T(8,128)(2,1)}, bf16[336,768]{1,0:T(8,128)(2,1)}, bf16[4,320,768]{2,1,0:T(8,128)(2,1)}, bf16[4,320,768]{2,1,0:T(8,128)(2,1)}) custom-call(s32[1]{0:T(128)} %bitcast.6.refs_0_, bf16[4,320,768]{2,1,0:T(8,128)(2,1)} %all-gather.7.cloned.1.call-done.refs_1_, ...), custom_call_target="tpu_custom_call", output_to_operand_aliasing={{2}: (5, {}), {3}: (6, {})} | custom-call | flops 15099494 | bytes 100000 | tf_op jit(solution)/shard_map/experts/pallas_call | solution.py:794
  139.1 11.1 %expert_weights.2 = (f32[2,768,768]{2,1,0:T(8,128)}, f32[2,768,768]{2,1,0:T(8,128)}, bf16[4,8,2,40,768]{4,3,2,1,0:T(8,128)(2,1)}) custom-call(s32[1]{0:T(128)} %bitcast.3.refs_0_, bf16[4,320,768]{2,1,0:T(8,128)(2,1)} %all-gather.7.cloned.1.call-done.refs_1_, bf16[4,320,768]{2,1,0:T(8,128)(2,1)} %bitcast.110, ...), custom_call_target="tpu_custom_call" | custom-call | flops 30198988 | bytes 130000 | tf_op jit(solution)/shard_map/expert_weights/pallas_call | solution.py:841
  153.0 5.2 %collective-permute-start.7 = (bf16[336,768]{1,0:T(8,128)(2,1)S(1)}, bf16[336,768]{1,0:T(8,128)(2,1)S(1)}, u32[]{:S(2)}, u32[]{:S(2)}) collective-permute-start(bf16[336,768]{1,0:T(8,128)(2,1)S(1)} %get-tuple-element.127), channel_id=1, source_target_pairs={{0,1},{1,2},{4,5},{5,6},{8,9},{9,10},{12,13},{13,14},{16,17},{17,1... | collective-permute-start | bytes 1548296 | tf_op jit(solution)/shard_map/ppermute | solution.py:589
  158.2 20.4 %collective-permute-done.8 = bf16[336,768]{1,0:T(8,128)(2,1)S(1)} collective-permute-done((bf16[336,768]{1,0:T(8,128)(2,1)S(1)}, bf16[336,768]{1,0:T(8,128)(2,1)S(1)}, u32[]{:S(2)}, u32[]{:S(2)}) %collective-permute-start.8) | collective-permute-done | bytes 516128 | tf_op jit(solution)/shard_map/ppermute | solution.py:591
  186.1 7.1 %experts.6 = (bf16[336,768]{1,0:T(8,128)(2,1)}, bf16[336,768]{1,0:T(8,128)(2,1)}, bf16[4,320,768]{2,1,0:T(8,128)(2,1)}, bf16[4,320,768]{2,1,0:T(8,128)(2,1)}) custom-call(s32[1]{0:T(128)} %bitcast.6.refs_0_, bf16[4,320,768]{2,1,0:T(8,128)(2,1)} %all-gather.5.cloned.1.call-done.refs_1_, bf16[4,320,768]{2,1,0:T(8,128)(2,1)} %bitcast.105, ...), custom_call_target="tpu_custom_call" | custom-call | flops 15099494 | bytes 100000 | tf_op jit(solution)/shard_map/experts/pallas_call | solution.py:794
  195.3 7.2 %experts.7 = (bf16[336,768]{1,0:T(8,128)(2,1)}, bf16[336,768]{1,0:T(8,128)(2,1)}, bf16[4,320,768]{2,1,0:T(8,128)(2,1)}, bf16[4,320,768]{2,1,0:T(8,128)(2,1)}) custom-call(s32[1]{0:T(128)} %bitcast.6.refs_0_, bf16[4,320,768]{2,1,0:T(8,128)(2,1)} %all-gather.5.cloned.1.call-done.refs_1_, ...), custom_call_target="tpu_custom_call", output_to_operand_aliasing={{2}: (5, {}), {3}: (6, {})} | custom-call | flops 15099494 | bytes 100000 | tf_op jit(solution)/shard_map/experts/pallas_call | solution.py:794
  209.3 5.1 %collective-permute-start.9 = (bf16[336,768]{1,0:T(8,128)(2,1)S(1)}, bf16[336,768]{1,0:T(8,128)(2,1)S(1)}, u32[]{:S(2)}, u32[]{:S(2)}) collective-permute-start(bf16[336,768]{1,0:T(8,128)(2,1)S(1)} %get-tuple-element.129), channel_id=1, source_target_pairs={{0,1},{1,2},{4,5},{5,6},{8,9},{9,10},{12,13},{13,14},{16,17},{17,1... | collective-permute-start | bytes 1548296 | tf_op jit(solution)/shard_map/ppermute | solution.py:589
  215.3 8.0 %all-to-all-start.4 = ((bf16[8,48,768]{2,1,0:T(8,128)(2,1)}), bf16[8,48,768]{2,1,0:T(8,128)(2,1)S(1)}, u32[]{:S(2)}, u32[]{:S(2)}) async-start(bf16[8,48,768]{2,1,0:T(8,128)(2,1)} %fusion.14), calls=%async_computation.5 | async-start | bytes 1179648 | tf_op jit(solution)/shard_map/all_to_all | solution.py:696
  230.0 11.1 %expert_weights.3 = (f32[2,768,768]{2,1,0:T(8,128)}, f32[2,768,768]{2,1,0:T(8,128)}, bf16[4,8,2,40,768]{4,3,2,1,0:T(8,128)(2,1)}) custom-call(s32[1]{0:T(128)} %bitcast.3.refs_0_, bf16[4,320,768]{2,1,0:T(8,128)(2,1)} %all-gather.5.cloned.1.call-done.refs_1_, ...), custom_call_target="tpu_custom_call", output_to_operand_aliasing={{0}: (7, {}), {1}: (8, {}), {2}: (9, {})} | custom-call | flops 30198988 | bytes 130000 | tf_op jit(solution)/shard_map/expert_weights/pallas_call | solution.py:841
  243.5 7.0 %all-to-all-start.5 = ((bf16[8,48,768]{2,1,0:T(8,128)(2,1)}), bf16[8,48,768]{2,1,0:T(8,128)(2,1)S(1)}, u32[]{:S(2)}, u32[]{:S(2)}) async-start(bf16[8,48,768]{2,1,0:T(8,128)(2,1)} %fusion.15), calls=%async_computation.6 | async-start | bytes 1179648 | tf_op jit(solution)/shard_map/all_to_all | solution.py:696
  250.5 7.0 %all-to-all-done.5 = bf16[8,48,768]{2,1,0:T(8,128)(2,1)S(1)} async-done(((bf16[8,48,768]{2,1,0:T(8,128)(2,1)}), bf16[8,48,768]{2,1,0:T(8,128)(2,1)S(1)}, u32[]{:S(2)}, u32[]{:S(2)}) %all-to-all-start.5) | async-done | bytes 589856 | tf_op jit(solution)/shard_map/all_to_all | solution.py:696
  258.4 8.8 %middle.1 = (f32[512,768]{1,0:T(8,128)}, bf16[512,768]{1,0:T(8,128)(2,1)}, bf16[512,768]{1,0:T(8,128)(2,1)}, bf16[768,128]{1,0:T(8,128)(2,1)}) custom-call(f32[512,768]{1,0:T(8,128)} %get-tuple-element.101.residual_ref, bf16[512,768]{1,0:T(8,128)(2,1)} %cot_ref.1, f32[1,768]{1,0:T(1,128)} %broadcast_in_dim.19.gain_ref, f32[768,16]{1,0:T(8,128)} %copy.47.w_router_ref.refs_4_, ...), custom_call_target="tpu_custom_call" | custom-call | flops 60000000 | bytes 80000 | tf_op jit(solution)/shard_map/middle/pallas_call | solution.py:944
  267.2 10.0 %attend_back.3 = (bf16[512,256]{1,0:T(8,128)(2,1)}, bf16[512,256]{1,0:T(8,128)(2,1)}, bf16[512,256]{1,0:T(8,128)(2,1)}, bf16[768,1664]{1,0:T(8,128)(2,1)}, f32[16,768]{1,0:T(8,128)}) custom-call(bf16[512,2304]{1,0:T(8,128)(2,1)} %get-tuple-element.95.q_ref.k_ref.v_ref, bf16[512,2304]{1,0:T(8,128)(2,1)} %get-tuple-element.95.q_ref.k_ref.v_ref, ...), custom_call_target="tpu_custom_call" | custom-call | flops 80000000 | bytes 60000 | tf_op jit(solution)/shard_map/attend_back/pallas_call | solution.py:999
  282.0 5.1 %attend_back.4 = (bf16[512,128]{1,0:T(8,128)(2,1)}, bf16[512,128]{1,0:T(8,128)(2,1)}, bf16[512,128]{1,0:T(8,128)(2,1)}, bf16[768,384]{1,0:T(8,128)(2,1)}, f32[16,768]{1,0:T(8,128)}) custom-call(bf16[512,2304]{1,0:T(8,128)(2,1)} %get-tuple-element.95.q_ref.k_ref.v_ref, bf16[512,2304]{1,0:T(8,128)(2,1)} %get-tuple-element.95.q_ref.k_ref.v_ref, ...), custom_call_target="tpu_custom_call" | custom-call | flops 40000000 | bytes 30000 | tf_op jit(solution)/shard_map/attend_back/pallas_call | solution.py:999
  290.2 12.2 %attend_back.5 = (bf16[512,384]{1,0:T(8,128)(2,1)}, bf16[512,384]{1,0:T(8,128)(2,1)}, bf16[512,384]{1,0:T(8,128)(2,1)}, bf16[768,1664]{1,0:T(8,128)(2,1)}, f32[16,768]{1,0:T(8,128)}) custom-call(bf16[512,2304]{1,0:T(8,128)(2,1)} %get-tuple-element.95.q_ref.k_ref.v_ref, bf16[512,2304]{1,0:T(8,128)(2,1)} %get-tuple-element.95.q_ref.k_ref.v_ref, ...), custom_call_target="tpu_custom_call" | custom-call | flops 120000000 | bytes 90000 | tf_op jit(solution)/shard_map/attend_back/pallas_call | solution.py:999
  319.5 6.4 %collective-permute-done.32 = bf16[96,1664]{1,0:T(8,128)(2,1)S(1)} collective-permute-done((bf16[96,1664]{1,0:T(8,128)(2,1)S(1)}, bf16[96,1664]{1,0:T(8,128)(2,1)S(1)}, u32[]{:S(2)}, u32[]{:S(2)}) %collective-permute-start.32) | collective-permute-done | bytes 319520 | tf_op jit(solution)/shard_map/ppermute | solution.py:636
  333.6 6.6 %all-to-all-start.3 = ((bf16[8,2,40,768]{3,2,1,0:T(8,128)(2,1)}), bf16[8,2,40,768]{3,2,1,0:T(8,128)(2,1)S(1)}, u32[]{:S(2)}, u32[]{:S(2)}) async-start(bf16[8,2,40,768]{3,2,1,0:T(8,128)(2,1)} %bitcast.143), calls=%async_computation.4 | async-start | bytes 1966080 | tf_op jit(solution)/shard_map/all_to_all | solution.py:696
  348.4 7.4 %tokens_grad.1 = f32[512,768]{1,0:T(8,128)} custom-call(bf16[512,768]{1,0:T(8,128)(2,1)} %refs_0_.1, f32[1,768]{1,0:T(1,128)} %broadcast_in_dim.15.gain_ref.refs_1_, bf16[768,2304]{1,0:T(8,128)(2,1)} %refs_2_.1, f32[512,768]{1,0:T(8,128)} %get-tuple-element.144.refs_3_, bf16[512,256]{1,0:T(8,128)(2,1)} %get-tuple-element.150.refs_4_, ...), custom_call_target="tpu_custom_call" | custom-call | flops 30000000 | bytes 100000 | tf_op jit(solution)/shard_map/tokens_grad/pallas_call | solution.py:1045
  361.3 6.6 %collective-permute-done.28 = bf16[4,24,1664]{2,1,0:T(8,128)(2,1)S(1)} collective-permute-done((bf16[4,24,1664]{2,1,0:T(8,128)(2,1)S(1)}, bf16[4,24,1664]{2,1,0:T(8,128)(2,1)S(1)}, u32[]{:S(2)}, u32[]{:S(2)}) %collective-permute-start.28) | collective-permute-done | bytes 319520 | tf_op jit(solution)/shard_map/ppermute | solution.py:660
  373.8 7.8 %collective-permute-done.41 = bf16[4,24,1664]{2,1,0:T(8,128)(2,1)S(1)} collective-permute-done((bf16[4,24,1664]{2,1,0:T(8,128)(2,1)S(1)}, bf16[4,24,1664]{2,1,0:T(8,128)(2,1)S(1)}, u32[]{:S(2)}, u32[]{:S(2)}) %collective-permute-start.41) | collective-permute-done | bytes 319520 | tf_op jit(solution)/shard_map/ppermute | solution.py:660
  383.3 5.8 %finish.2 = (f32[8,4,24,2304]{3,2,1,0:T(8,128)}, f32[8,4,24,768]{3,2,1,0:T(8,128)}, f32[8,4,24,128]{3,2,1,0:T(8,128)}, f32[8,4,24,256]{3,2,1,0:T(8,128)}) custom-call(s32[3]{0:T(128)} %pad_add_fusion.where_ref, bf16[4,4,24,1664]{3,2,1,0:T(8,128)(2,1)} %copy-done.1, bf16[4,4,24,1664]{3,2,1,0:T(8,128)(2,1)} %copy-done.2, bf16[8,4,24,2304]{3,2,1,0:T(8,128)(2,1)} %bitcast.103), custom_call_target="tpu_custom_call" | custom-call | flops 1000000 | bytes 100000 | tf_op jit(solution)/shard_map/finish/pallas_call | solution.py:1083
  390.7 5.8 %finish.3 = (f32[8,4,24,2304]{3,2,1,0:T(8,128)}, f32[8,4,24,768]{3,2,1,0:T(8,128)}, f32[8,4,24,128]{3,2,1,0:T(8,128)}, f32[8,4,24,256]{3,2,1,0:T(8,128)}) custom-call(s32[3]{0:T(128)} %pad_add_fusion.where_ref, bf16[4,4,24,1664]{3,2,1,0:T(8,128)(2,1)} %copy-done.8, ...), custom_call_target="tpu_custom_call", output_to_operand_aliasing={{0}: (4, {}), {1}: (5, {}), {2}: (6, {}), {3}: (7, {})} | custom-call | flops 1000000 | bytes 100000 | tf_op jit(solution)/shard_map/finish/pallas_call | solution.py:1083
  (188 shorter events, 122.8 us)
Async XLA Ops:
  7.2 65.7 %all-gather.9.cloned.1.call-start = ((), (), s32[]{:S(2)}) async-start(), calls=%async_computation.10 | async-start | bytes 3932160 | tf_op jit(solution)/shard_map/all_gather | solution.py:698
  7.9 110.5 %all-gather.7.cloned.1.call-start = ((), (), s32[]{:S(2)}) async-start(), calls=%async_computation.8 | async-start | bytes 2457600 | tf_op jit(solution)/shard_map/all_gather | solution.py:901
  77.3 26.3 %all-to-all-start.1 = ((bf16[8,4,40,768]{3,2,1,0:T(8,128)(2,1)}), bf16[8,4,40,768]{3,2,1,0:T(8,128)(2,1)S(1)}, u32[]{:S(2)}, u32[]{:S(2)}) async-start(bf16[8,4,40,768]{3,2,1,0:T(8,128)(2,1)} %slots.2.refs_6_), calls=%async_computation.1 | async-start | bytes 3932160 | tf_op jit(solution)/shard_map/all_to_all | solution.py:696
  81.8 104.4 %all-gather.5.cloned.1.call-start = ((), (), s32[]{:S(2)}) async-start(), calls=%async_computation.7 | async-start | bytes 2457600 | tf_op jit(solution)/shard_map/all_gather | solution.py:901
  125.5 26.0 %collective-permute-start.5 = (bf16[336,768]{1,0:T(8,128)(2,1)}, bf16[336,768]{1,0:T(8,128)(2,1)S(1)}, u32[]{:S(2)}, u32[]{:S(2)}) collective-permute-start(bf16[336,768]{1,0:T(8,128)(2,1)} %get-tuple-element.125), channel_id=1, source_target_pairs={{0,1},{4,5},{8,9},{12,13},{16,17},{20,21},{24,25},{28,29}} | collective-permute-start | bytes 1548296 | tf_op jit(solution)/shard_map/ppermute | solution.py:589
  126.8 24.7 %collective-permute-start.6 = (bf16[336,768]{1,0:T(8,128)(2,1)}, bf16[336,768]{1,0:T(8,128)(2,1)S(1)}, u32[]{:S(2)}, u32[]{:S(2)}) collective-permute-start(bf16[336,768]{1,0:T(8,128)(2,1)} %get-tuple-element.126), channel_id=1, source_target_pairs={{3,2},{7,6},{11,10},{15,14},{19,18},{23,22},{27,26},{31,30}} | collective-permute-start | bytes 1548296 | tf_op jit(solution)/shard_map/ppermute | solution.py:591
  127.5 57.3 %all-to-all-start.2 = ((bf16[8,4,40,768]{3,2,1,0:T(8,128)(2,1)}), bf16[8,4,40,768]{3,2,1,0:T(8,128)(2,1)S(1)}, u32[]{:S(2)}, u32[]{:S(2)}) async-start(bf16[8,4,40,768]{3,2,1,0:T(8,128)(2,1)} %slots.3.refs_5_), calls=%async_computation.2 | async-start | bytes 3932160 | tf_op jit(solution)/shard_map/all_to_all | solution.py:696
  151.7 26.9 %collective-permute-start.8 = (bf16[336,768]{1,0:T(8,128)(2,1)S(1)}, bf16[336,768]{1,0:T(8,128)(2,1)S(1)}, u32[]{:S(2)}, u32[]{:S(2)}) collective-permute-start(bf16[336,768]{1,0:T(8,128)(2,1)S(1)} %get-tuple-element.128), channel_id=1, source_target_pairs={{2,1},{3,2},{6,5},{7,6},{10,9},{11,10},{14,13},{15,14},{18,17},{19... | collective-permute-start | bytes 1548296 | tf_op jit(solution)/shard_map/ppermute | solution.py:591
  153.0 25.9 %collective-permute-start.7 = (bf16[336,768]{1,0:T(8,128)(2,1)S(1)}, bf16[336,768]{1,0:T(8,128)(2,1)S(1)}, u32[]{:S(2)}, u32[]{:S(2)}) collective-permute-start(bf16[336,768]{1,0:T(8,128)(2,1)S(1)} %get-tuple-element.127), channel_id=1, source_target_pairs={{0,1},{1,2},{4,5},{5,6},{8,9},{9,10},{12,13},{13,14},{16,17},{17,1... | collective-permute-start | bytes 1548296 | tf_op jit(solution)/shard_map/ppermute | solution.py:589
  179.0 16.2 %collective-permute-start.10 = (bf16[336,768]{1,0:T(8,128)(2,1)S(1)}, bf16[336,768]{1,0:T(8,128)(2,1)S(1)}, u32[]{:S(2)}, u32[]{:S(2)}) collective-permute-start(bf16[336,768]{1,0:T(8,128)(2,1)S(1)} %add_convert_fusion.5), channel_id=1, source_target_pairs={{0,1},{1,2},{2,3},{4,5},{5,6},{6,7},{8,9},{9,10},{10,11},{12,13},{... | collective-permute-start | bytes 1548296 | tf_op jit(solution)/shard_map/ppermute | solution.py:589
  206.7 16.6 %collective-permute-start.12 = (bf16[336,768]{1,0:T(8,128)(2,1)S(1)}, bf16[336,768]{1,0:T(8,128)(2,1)}, u32[]{:S(2)}, u32[]{:S(2)}) collective-permute-start(bf16[336,768]{1,0:T(8,128)(2,1)S(1)} %get-tuple-element.137), channel_id=1, source_target_pairs={{2,1},{3,2},{6,5},{7,6},{10,9},{11,10},{14,13},{15,14},{18,17},{19... | collective-permute-start | bytes 1548296 | tf_op jit(solution)/shard_map/ppermute | solution.py:591
  209.3 15.2 %collective-permute-start.9 = (bf16[336,768]{1,0:T(8,128)(2,1)S(1)}, bf16[336,768]{1,0:T(8,128)(2,1)S(1)}, u32[]{:S(2)}, u32[]{:S(2)}) collective-permute-start(bf16[336,768]{1,0:T(8,128)(2,1)S(1)} %get-tuple-element.129), channel_id=1, source_target_pairs={{0,1},{1,2},{4,5},{5,6},{8,9},{9,10},{12,13},{13,14},{16,17},{17,1... | collective-permute-start | bytes 1548296 | tf_op jit(solution)/shard_map/ppermute | solution.py:589
  215.3 25.8 %all-to-all-start.4 = ((bf16[8,48,768]{2,1,0:T(8,128)(2,1)}), bf16[8,48,768]{2,1,0:T(8,128)(2,1)S(1)}, u32[]{:S(2)}, u32[]{:S(2)}) async-start(bf16[8,48,768]{2,1,0:T(8,128)(2,1)} %fusion.14), calls=%async_computation.5 | async-start | bytes 1179648 | tf_op jit(solution)/shard_map/all_to_all | solution.py:696
  223.3 110.3 %reduce-scatter.2.cloned.1.call-start = ((), (), s32[]{:S(2)}) async-start(), calls=%async_computation.9 | async-start | bytes 4915200 | tf_op jit(solution)/shard_map/reduce_scatter | solution.py:984
  224.7 16.5 %collective-permute-start.13 = (bf16[336,768]{1,0:T(8,128)(2,1)S(1)}, bf16[336,768]{1,0:T(8,128)(2,1)S(1)}, u32[]{:S(2)}, u32[]{:S(2)}) collective-permute-start(bf16[336,768]{1,0:T(8,128)(2,1)S(1)} %add_convert_fusion.2), channel_id=1, source_target_pairs={{0,1},{1,2},{2,3},{4,5},{5,6},{6,7},{8,9},{9,10},{10,11},{12,13},{... | collective-permute-start | bytes 1548296 | tf_op jit(solution)/shard_map/ppermute | solution.py:589
  226.6 14.6 %collective-permute-start.14 = (bf16[336,768]{1,0:T(8,128)(2,1)S(1)}, bf16[336,768]{1,0:T(8,128)(2,1)S(1)}, u32[]{:S(2)}, u32[]{:S(2)}) collective-permute-start(bf16[336,768]{1,0:T(8,128)(2,1)S(1)} %add_convert_fusion.1), channel_id=1, source_target_pairs={{1,0},{2,1},{3,2},{5,4},{6,5},{7,6},{9,8},{10,9},{11,10},{13,12},{... | collective-permute-start | bytes 1548296 | tf_op jit(solution)/shard_map/ppermute | solution.py:591
  243.5 14.0 %all-to-all-start.5 = ((bf16[8,48,768]{2,1,0:T(8,128)(2,1)}), bf16[8,48,768]{2,1,0:T(8,128)(2,1)S(1)}, u32[]{:S(2)}, u32[]{:S(2)}) async-start(bf16[8,48,768]{2,1,0:T(8,128)(2,1)} %fusion.15), calls=%async_computation.6 | async-start | bytes 1179648 | tf_op jit(solution)/shard_map/all_to_all | solution.py:696
  287.5 14.9 %collective-permute-start.16 = (bf16[96,1664]{1,0:T(8,128)(2,1)S(1)}, bf16[96,1664]{1,0:T(8,128)(2,1)S(1)}, u32[]{:S(2)}, u32[]{:S(2)}) collective-permute-start(bf16[96,1664]{1,0:T(8,128)(2,1)S(1)} %get-tuple-element.185), channel_id=1, source_target_pairs={{0,8},{4,12},{8,0},{12,4},{16,24},{20,28},{24,16},{28,20},{1,9},{5... | collective-permute-start | bytes 958472 | tf_op jit(solution)/shard_map/ppermute | solution.py:636
  287.9 14.5 %collective-permute-start.17 = (bf16[96,1664]{1,0:T(8,128)(2,1)S(1)}, bf16[96,1664]{1,0:T(8,128)(2,1)S(1)}, u32[]{:S(2)}, u32[]{:S(2)}) collective-permute-start(bf16[96,1664]{1,0:T(8,128)(2,1)S(1)} %get-tuple-element.187), channel_id=1, source_target_pairs={{0,16},{4,20},{8,24},{12,28},{16,0},{20,4},{24,8},{28,12},{1,17},{... | collective-permute-start | bytes 958472 | tf_op jit(solution)/shard_map/ppermute | solution.py:636
  288.3 15.3 %collective-permute-start.18 = (bf16[96,1664]{1,0:T(8,128)(2,1)S(1)}, bf16[96,1664]{1,0:T(8,128)(2,1)S(1)}, u32[]{:S(2)}, u32[]{:S(2)}) collective-permute-start(bf16[96,1664]{1,0:T(8,128)(2,1)S(1)} %get-tuple-element.186), channel_id=1, source_target_pairs={{0,24},{4,28},{8,16},{12,20},{16,8},{20,12},{24,0},{28,4},{1,25},{... | collective-permute-start | bytes 958472 | tf_op jit(solution)/shard_map/ppermute | solution.py:636
  311.1 14.8 %collective-permute-start.32 = (bf16[96,1664]{1,0:T(8,128)(2,1)S(1)}, bf16[96,1664]{1,0:T(8,128)(2,1)S(1)}, u32[]{:S(2)}, u32[]{:S(2)}) collective-permute-start(bf16[96,1664]{1,0:T(8,128)(2,1)S(1)} %get-tuple-element.183), channel_id=1, source_target_pairs={{0,24},{4,28},{8,16},{12,20},{16,8},{20,12},{24,0},{28,4},{1,25},{... | collective-permute-start | bytes 958472 | tf_op jit(solution)/shard_map/ppermute | solution.py:636
  312.4 15.6 %collective-permute-start.20 = (bf16[24,1664]{1,0:T(8,128)(2,1)S(1)}, bf16[24,1664]{1,0:T(8,128)(2,1)S(1)}, u32[]{:S(2)}, u32[]{:S(2)}) collective-permute-start(bf16[24,1664]{1,0:T(8,128)(2,1)S(1)} %get-tuple-element.199), channel_id=1, source_target_pairs={{0,1},{1,2},{2,3},{3,0},{4,5},{5,6},{6,7},{7,4},{8,9},{9,10},{10,1... | collective-permute-start | bytes 239624 | tf_op jit(solution)/shard_map/ppermute | solution.py:645
  314.2 15.0 %collective-permute-start.21 = (bf16[24,1664]{1,0:T(8,128)(2,1)S(1)}, bf16[24,1664]{1,0:T(8,128)(2,1)S(1)}, u32[]{:S(2)}, u32[]{:S(2)}) collective-permute-start(bf16[24,1664]{1,0:T(8,128)(2,1)S(1)} %get-tuple-element.201), channel_id=1, source_target_pairs={{0,2},{1,3},{2,0},{3,1},{4,6},{5,7},{6,4},{7,5},{8,10},{9,11},{10,... | collective-permute-start | bytes 239624 | tf_op jit(solution)/shard_map/ppermute | solution.py:645
  326.1 14.1 %collective-permute-start.33 = (bf16[24,1664]{1,0:T(8,128)(2,1)S(1)}, bf16[24,1664]{1,0:T(8,128)(2,1)S(1)}, u32[]{:S(2)}, u32[]{:S(2)}) collective-permute-start(bf16[24,1664]{1,0:T(8,128)(2,1)S(1)} %get-tuple-element.194), channel_id=1, source_target_pairs={{0,1},{1,2},{2,3},{3,0},{4,5},{5,6},{6,7},{7,4},{8,9},{9,10},{10,1... | collective-permute-start | bytes 239624 | tf_op jit(solution)/shard_map/ppermute | solution.py:645
  333.6 22.2 %all-to-all-start.3 = ((bf16[8,2,40,768]{3,2,1,0:T(8,128)(2,1)}), bf16[8,2,40,768]{3,2,1,0:T(8,128)(2,1)S(1)}, u32[]{:S(2)}, u32[]{:S(2)}) async-start(bf16[8,2,40,768]{3,2,1,0:T(8,128)(2,1)} %bitcast.143), calls=%async_computation.4 | async-start | bytes 1966080 | tf_op jit(solution)/shard_map/all_to_all | solution.py:696
  344.2 15.9 %collective-permute-start.26 = (bf16[4,24,1664]{2,1,0:T(8,128)(2,1)S(1)}, bf16[4,24,1664]{2,1,0:T(8,128)(2,1)S(1)}, u32[]{:S(2)}, u32[]{:S(2)}) collective-permute-start(bf16[4,24,1664]{2,1,0:T(8,128)(2,1)S(1)} %get-tuple-element.198), channel_id=1, source_target_pairs={{0,8},{4,12},{8,0},{12,4},{16,24},{20,28},{24,16},{28,20},{1,9},{5... | collective-permute-start | bytes 958472 | tf_op jit(solution)/shard_map/ppermute | solution.py:660
  346.9 14.4 %collective-permute-start.27 = (bf16[4,24,1664]{2,1,0:T(8,128)(2,1)S(1)}, bf16[4,24,1664]{2,1,0:T(8,128)(2,1)S(1)}, u32[]{:S(2)}, u32[]{:S(2)}) collective-permute-start(bf16[4,24,1664]{2,1,0:T(8,128)(2,1)S(1)} %get-tuple-element.198), channel_id=1, source_target_pairs={{0,16},{4,20},{8,24},{12,28},{16,0},{20,4},{24,8},{28,12},{1,17},{... | collective-permute-start | bytes 958472 | tf_op jit(solution)/shard_map/ppermute | solution.py:660
  348.1 19.8 %collective-permute-start.28 = (bf16[4,24,1664]{2,1,0:T(8,128)(2,1)S(1)}, bf16[4,24,1664]{2,1,0:T(8,128)(2,1)S(1)}, u32[]{:S(2)}, u32[]{:S(2)}) collective-permute-start(bf16[4,24,1664]{2,1,0:T(8,128)(2,1)S(1)} %get-tuple-element.198), channel_id=1, source_target_pairs={{0,24},{4,28},{8,16},{12,20},{16,8},{20,12},{24,0},{28,4},{1,25},{... | collective-permute-start | bytes 958472 | tf_op jit(solution)/shard_map/ppermute | solution.py:660
  356.8 17.0 %collective-permute-start.39 = (bf16[4,24,1664]{2,1,0:T(8,128)(2,1)S(1)}, bf16[4,24,1664]{2,1,0:T(8,128)(2,1)S(1)}, u32[]{:S(2)}, u32[]{:S(2)}) collective-permute-start(bf16[4,24,1664]{2,1,0:T(8,128)(2,1)S(1)} %pad_maximum_fusion.3), channel_id=1, source_target_pairs={{0,8},{4,12},{8,0},{12,4},{16,24},{20,28},{24,16},{28,20},{1,9},{5... | collective-permute-start | bytes 958472 | tf_op jit(solution)/shard_map/ppermute | solution.py:660
  358.0 15.8 %collective-permute-start.40 = (bf16[4,24,1664]{2,1,0:T(8,128)(2,1)S(1)}, bf16[4,24,1664]{2,1,0:T(8,128)(2,1)S(1)}, u32[]{:S(2)}, u32[]{:S(2)}) collective-permute-start(bf16[4,24,1664]{2,1,0:T(8,128)(2,1)S(1)} %pad_maximum_fusion.3), channel_id=1, source_target_pairs={{0,16},{4,20},{8,24},{12,28},{16,0},{20,4},{24,8},{28,12},{1,17},{... | collective-permute-start | bytes 958472 | tf_op jit(solution)/shard_map/ppermute | solution.py:660
  360.1 21.5 %collective-permute-start.41 = (bf16[4,24,1664]{2,1,0:T(8,128)(2,1)S(1)}, bf16[4,24,1664]{2,1,0:T(8,128)(2,1)S(1)}, u32[]{:S(2)}, u32[]{:S(2)}) collective-permute-start(bf16[4,24,1664]{2,1,0:T(8,128)(2,1)S(1)} %pad_maximum_fusion.3), channel_id=1, source_target_pairs={{0,24},{4,28},{8,16},{12,20},{16,8},{20,12},{24,0},{28,4},{1,25},{... | collective-permute-start | bytes 958472 | tf_op jit(solution)/shard_map/ppermute | solution.py:660
  368.1 21.1 %collective-permute-start.29 = (bf16[4,4,24,1664]{3,2,1,0:T(8,128)(2,1)S(1)}, bf16[4,4,24,1664]{3,2,1,0:T(8,128)(2,1)S(1)}, u32[]{:S(2)}, u32[]{:S(2)}) collective-permute-start(bf16[4,4,24,1664]{3,2,1,0:T(8,128)(2,1)S(1)} %pad_maximum_fusion.a_ref), channel_id=1, source_target_pairs={{0,4},{4,0},{8,12},{12,8},{16,20},{20,16},{24,28},{28,24},{1,5},{5... | collective-permute-start | bytes 3833864 | tf_op jit(solution)/shard_map/ppermute | solution.py:664
  (43 other events, 349.1 us)
Sparse Core Ops, SparseCore 0:
  9.6 63.2 all-gather.8
  75.0 43.3 all-gather.6
  120.0 64.5 all-gather.4
  241.2 75.6 reduce-scatter.1
